TPU v7x, 256 devices: a whole 4x4x8 slice. The times are simulated.
256 devices in a mesh: tm: 32 (over x, z), height: 4 (over y_hi, core), heads: 2 (over y_lo).
Axes of the slice: x: 4, y: 4 (y_hi: 2, y_lo: 2; y = y_hi * 2 + y_lo), z: 8, core: 2. Of those that a mesh axis runs over, the one named last changes fastest.
Arguments:
- queries: bfloat16 [192, 32, 8, 768], P('tm', 'height', None, 'heads'), may hold values from -18 to 18
- key_tokens: bfloat16 [192, 32, 8, 768], P('tm', 'height', None, 'heads'), may hold values from -4 to 4
- value_tokens: bfloat16 [192, 32, 8, 768], P('tm', 'height', None, 'heads'), may hold values from -5 to 5
- cotangent: bfloat16 [192, 32, 8, 768], P('tm', 'height', None, 'heads'), may hold values from -5 to 5
- window_mask: int32 [32, 4, 9], replicated, may hold values 0 or 1
Outputs:
- attended: bfloat16 [192, 32, 8, 768], P('tm', 'height', None, 'heads')
- query_grad: bfloat16 [192, 32, 8, 768], P('tm', 'height', None, 'heads')
- key_grad: bfloat16 [192, 32, 8, 768], P('tm', 'height', None, 'heads')
- value_grad: bfloat16 [192, 32, 8, 768], P('tm', 'height', None, 'heads')
All inputs are finite; a program needn't handle non-finite values.
Results may differ from a plain program's by a relative error of at most 0.012.
Values may be sent and summed in bfloat16 or wider, within the bound.
A program may use at most 128 MiB of HBM per device.

v0:
```python
import jax
import jax.numpy as jnp
from jax import lax
from jax.sharding import PartitionSpec as P

HEAD_DIM = 64
TILE_T = 6


masked_score = -1e30


def passed_along(array, axis, by):
    peers = lax.axis_size(axis)
    pairs = [(i, i + by) for i in range(peers) if 0 <= i + by < peers]
    return lax.ppermute(array, axis, pairs)


def padded(block, sides, width):
    for axis, dim in sides:
        count = lax.axis_size(axis)
        forward = [(i, i + 1) for i in range(count - 1)]
        backward = [(target, source) for source, target in forward]
        low = lax.ppermute(
            lax.slice_in_dim(block, block.shape[dim] - width, None, axis=dim), axis, forward
        )
        high = lax.ppermute(lax.slice_in_dim(block, 0, width, axis=dim), axis, backward)
        block = jnp.concatenate([low, block, high], axis=dim)
    return block


def head_slice(tiles, head):
    return lax.dynamic_slice_in_dim(tiles, head * HEAD_DIM, HEAD_DIM, axis=tiles.ndim - 1)


def put_head(buffer, piece, head):
    return lax.dynamic_update_slice_in_dim(buffer, piece, head * HEAD_DIM, axis=buffer.ndim - 1)


def window_of(extended, tile_count):
    pieces = [
        extended[:, time_move : time_move + tile_count, height_move]
        for time_move in range(3)
        for height_move in range(3)
    ]
    stacked = jnp.stack(pieces, axis=2)
    return stacked.reshape(stacked.shape[:2] + (9 * stacked.shape[3], stacked.shape[4]))


def query_head(inputs, usable):
    query_rows, key_rows, value_rows, grad_rows = inputs
    scale = HEAD_DIM ** (-0.5)
    scores = (
        jnp.einsum("tqd,tkd->tqk", query_rows, key_rows, preferred_element_type=jnp.float32) * scale
    )
    scores = jnp.where(usable[:, None, :], scores, masked_score)
    highest = jnp.max(scores, axis=-1, keepdims=True)
    logsum = highest + jnp.log(jnp.sum(jnp.exp(scores - highest), axis=-1, keepdims=True))
    weights_low = jnp.exp(scores - logsum).astype(jnp.bfloat16)
    output = jnp.einsum(
        "tqk,tkd->tqd", weights_low, value_rows, preferred_element_type=jnp.float32
    ).astype(jnp.bfloat16)
    carried = jnp.sum(grad_rows.astype(jnp.float32) * output.astype(jnp.float32), axis=-1)
    product = jnp.einsum("tqd,tkd->tqk", grad_rows, value_rows, preferred_element_type=jnp.float32)
    slopes = (jnp.exp(scores - logsum) * (product - carried[:, :, None]) * scale).astype(
        jnp.bfloat16
    )
    query_grad = jnp.einsum(
        "tqk,tkd->tqd", slopes, key_rows, preferred_element_type=jnp.float32
    ).astype(jnp.bfloat16)
    results = (output, query_grad, logsum[:, :, 0], carried)
    value_part = jnp.einsum(
        "tqk,tqd->tkd", weights_low, grad_rows, preferred_element_type=jnp.float32
    )
    key_part = jnp.einsum("tqk,tqd->tkd", slopes, query_rows, preferred_element_type=jnp.float32)
    return results + (key_part, value_part)


def return_terms(partial_sums, tile_count):
    from_earlier = passed_along(
        partial_sums[:, tile_count + 1].astype(jnp.bfloat16), "tm", 1
    ).astype(jnp.float32)
    from_later = passed_along(partial_sums[:, 0].astype(jnp.bfloat16), "tm", -1).astype(jnp.float32)
    owned = partial_sums[:, 1 : tile_count + 1]
    owned = owned.at[:, 0].add(from_earlier).at[:, tile_count - 1].add(from_later)
    from_below = passed_along(owned[:, :, 2].astype(jnp.bfloat16), "height", 1).astype(jnp.float32)
    from_above = passed_along(owned[:, :, 0].astype(jnp.bfloat16), "height", -1).astype(jnp.float32)
    return owned[:, :, 1] + from_below + from_above


def local(queries, key_tokens, value_tokens, cotangent, window_mask):
    frames, height_rows, columns, features = queries.shape
    tile_count = frames // TILE_T
    tile_size = TILE_T * height_rows * columns
    head_count = features // HEAD_DIM
    tiles_shape = (tile_count, tile_size, features)
    query_tiles = queries.reshape(tiles_shape)
    key_tiles = key_tokens.reshape(tiles_shape)
    value_tiles = value_tokens.reshape(tiles_shape)
    grad_tiles = cotangent.reshape(tiles_shape)
    time_first_tile = lax.axis_index("tm") * tile_count
    height_here = lax.axis_index("height")
    tiles_total = tile_count * lax.axis_size("tm")
    height_total = lax.axis_size("height")
    offset = jnp.arange(9, dtype=jnp.int32)[None, :]
    own_mask = lax.dynamic_slice(
        window_mask, (time_first_tile, height_here, jnp.int32(0)), (tile_count, 1, 9)
    )[:, 0]
    time_index = (
        time_first_tile + jnp.arange(tile_count, dtype=jnp.int32)[:, None] + offset // 3 - 1
    )
    height_index = height_here + offset % 3 - 1
    inside = (
        (time_index >= 0)
        & (time_index < tiles_total)
        & (height_index >= 0)
        & (height_index < height_total)
    )
    allowed = inside & ((offset == 4) | (own_mask == 1))
    usable = jnp.repeat(allowed, tile_size, axis=1)
    output_init = jnp.zeros(tiles_shape, jnp.bfloat16)
    key_value = jnp.stack([key_tiles, value_tiles])[:, :, None]
    extended = padded(key_value, (("tm", 1), ("height", 2)), 1)
    neighbours = window_of(extended, tile_count)

    def forward_step(head, carry):
        output_all, query_all, collected = carry
        inputs = (
            head_slice(query_tiles, head),
            head_slice(neighbours[0], head),
            head_slice(neighbours[1], head),
            head_slice(grad_tiles, head),
        )
        output, query_grad, logsum, carried, key_part, value_part = query_head(inputs, usable)
        parts = jnp.stack([key_part, value_part]).reshape(
            (2, tile_count, 3, 3, tile_size, HEAD_DIM)
        )
        summed = jnp.zeros((2, tile_count + 2, 3, tile_size, HEAD_DIM), jnp.float32)
        for time_move in range(3):
            summed = summed + jnp.pad(
                parts[:, :, time_move], ((0, 0), (time_move, 2 - time_move), (0, 0), (0, 0), (0, 0))
            )
        return (
            put_head(output_all, output, head),
            put_head(query_all, query_grad, head),
            put_head(collected, summed, head),
        )

    collected_init = jnp.zeros((2, tile_count + 2, 3, tile_size, features), jnp.float32)
    output, query_grad, collected = lax.fori_loop(
        0, head_count, forward_step, (output_init, output_init, collected_init)
    )
    owned = return_terms(collected, tile_count)
    key_grad = owned[0]
    value_grad = owned[1]
    shape = queries.shape
    return (
        output.reshape(shape),
        query_grad.reshape(shape),
        key_grad.astype(jnp.bfloat16).reshape(shape),
        value_grad.astype(jnp.bfloat16).reshape(shape),
    )


def solution(mesh):
    in_specs = (
        P("tm", "height", None, "heads"),
        P("tm", "height", None, "heads"),
        P("tm", "height", None, "heads"),
        P("tm", "height", None, "heads"),
        P(),
    )
    out_specs = (
        P("tm", "height", None, "heads"),
        P("tm", "height", None, "heads"),
        P("tm", "height", None, "heads"),
        P("tm", "height", None, "heads"),
    )
    return jax.shard_map(local, mesh=mesh, in_specs=in_specs, out_specs=out_specs, check_vma=False)
```

profile of v0, /device:TPU:7, one launch (start us, length us, event | category | flops | bytes accessed | tf_op | source)
XLA Modules:
  0.0 298.7 jit_solution(5050584689416698427)
XLA Ops:
  1.8 7.8 %collective-permute-start.1 = (bf16[2,1,1,384,384]{4,3,2,0,1:T(8,128)(2,1)S(1)}, bf16[2,1,1,384,384]{4,3,2,0,1:T(8,128)(2,1)S(1)}, u32[]{:S(2)}, u32[]{:S(2)}) collective-permute-start(bf16[2,1,1,384,384]{4,3,2,0,1:T(8,128)(2,1)S(1)} %maximum_bitcast_fusion), channel_id=1, source_target_pairs={{8,0},{16,8},{24,16},{32,24},{40,32},{48,40},{56,48},{64,56},{72,6... | collective-permute-start | bytes 1769480 | tf_op jit(solution)/shard_map/ppermute | solution.py:27
  9.6 1.9 collective-permute-start
  11.5 10.0 %collective-permute-done.1 = bf16[2,1,1,384,384]{4,3,2,0,1:T(8,128)(2,1)S(1)} collective-permute-done((bf16[2,1,1,384,384]{4,3,2,0,1:T(8,128)(2,1)S(1)}, bf16[2,1,1,384,384]{4,3,2,0,1:T(8,128)(2,1)S(1)}, u32[]{:S(2)}, u32[]{:S(2)}) %collective-permute-start.1) | collective-permute-done | bytes 589856 | tf_op jit(solution)/shard_map/ppermute | solution.py:27
  21.6 5.9 %collective-permute-done = bf16[2,1,1,384,384]{4,3,2,0,1:T(8,128)(2,1)S(1)} collective-permute-done((bf16[2,1,1,384,384]{4,3,2,0,1:T(8,128)(2,1)S(1)}, bf16[2,1,1,384,384]{4,3,2,0,1:T(8,128)(2,1)S(1)}, u32[]{:S(2)}, u32[]{:S(2)}) %collective-permute-start) | collective-permute-done | bytes 589856 | tf_op jit(solution)/shard_map/ppermute | solution.py:24
  28.9 6.7 %collective-permute-start.2 = (bf16[2,3,1,384,384]{4,3,2,0,1:T(8,128)(2,1)}, bf16[2,3,1,384,384]{4,3,2,0,1:T(8,128)(2,1)}, u32[]{:S(2)}, u32[]{:S(2)}) collective-permute-start(bf16[2,3,1,384,384]{4,3,2,0,1:T(8,128)(2,1)} %pad_maximum_fusion.1), channel_id=1, source_target_pairs={{0,2},{2,4},{4,6},{1,3},{3,5},{5,7},{8,10},{10,12},{12,14},{9,11},... | collective-permute-start | bytes 5308424 | tf_op jit(solution)/shard_map/ppermute | solution.py:24
  35.6 1.9 collective-permute-start.3
  39.1 16.3 %collective-permute-done.2 = bf16[2,3,1,384,384]{4,3,2,0,1:T(8,128)(2,1)} collective-permute-done((bf16[2,3,1,384,384]{4,3,2,0,1:T(8,128)(2,1)}, bf16[2,3,1,384,384]{4,3,2,0,1:T(8,128)(2,1)}, u32[]{:S(2)}, u32[]{:S(2)}) %collective-permute-start.2) | collective-permute-done | bytes 1769504 | tf_op jit(solution)/shard_map/ppermute | solution.py:24
  55.4 1.9 slice_dynamic-update-slice_fusion.5
  58.2 3.1 %collective-permute-done.3 = bf16[2,3,1,384,384]{4,3,2,0,1:T(8,128)(2,1)} collective-permute-done((bf16[2,3,1,384,384]{4,3,2,0,1:T(8,128)(2,1)}, bf16[2,3,1,384,384]{4,3,2,0,1:T(8,128)(2,1)}, u32[]{:S(2)}, u32[]{:S(2)}) %collective-permute-start.3) | collective-permute-done | bytes 1769504 | tf_op jit(solution)/shard_map/ppermute | solution.py:27
  61.3 2.0 slice_dynamic-update-slice_fusion.4
  63.3 1.9 slice_dynamic-update-slice_fusion.3
  66.1 1.9 slice_dynamic-update-slice_fusion.2
  68.0 2.0 slice_dynamic-update-slice_fusion.1
  70.9 1.9 slice_dynamic-update-slice_fusion
  72.9 5.2 %broadcast_in_dim.45 = f32[2,3,3,384,384]{3,4,2,0,1:T(8,128)} broadcast(f32[]{:T(128)} %constant.168.clone.1), dimensions={} | broadcast | bytes 10616836 | tf_op jit(solution)/shard_map/broadcast_in_dim | solution.py:149
  78.1 164.1 %while.22 = (s32[]{:T(128)}, bf16[1,384,384]{1,2,0:T(8,128)(2,1)S(1)}, bf16[1,384,384]{1,2,0:T(8,128)(2,1)S(1)}, f32[2,3,3,384,384]{3,4,2,0,1:T(8,128)}, bf16[1,...) while((s32[]{:T(128)}, ...), condition=%wide.region_4.5_spmd.clone, body=%wide.region_0.4_spmd.clone.sunk | while | flops 1039269120 | bytes 83350048 | solution.py:150
  78.2 3.2 %fusion.75 = (bf16[1,1,3456,384]{3,2,1,0:T(8,128)(2,1)S(1)}, bf16[1,1,3456,384]{3,2,1,0:T(8,128)(2,1)S(1)}) fusion(bf16[2,1,3456,384]{3,2,1,0:T(8,128)(2,1)} %get-tuple-element.387), kind=kLoop, calls=%fused_computation.87.clone.1 | loop fusion | bytes 10616832 | tf_op jit(solution)/shard_map/while/body/eval_jaxpr/slice | solution.py:130
  87.4 2.3 fusion.79
  91.1 4.6 %copy.46 = bf16[3456,384]{1,0:T(8,128)(2,1)} copy(bf16[3456,384]{0,1:T(8,128)(2,1)} %fusion.79) | data formatting | bytes 5308416 | tf_op jit(solution)/shard_map/while/body/eval_jaxpr/convert_element_type | solution.py:59
  95.7 2.7 convolution_bitcast_fusion.5
  98.4 2.8 copy.45
  101.2 2.7 convolution_bitcast_fusion.4
  105.5 3.2 %fusion.75 = (bf16[1,1,3456,384]{3,2,1,0:T(8,128)(2,1)S(1)}, bf16[1,1,3456,384]{3,2,1,0:T(8,128)(2,1)S(1)}) fusion(bf16[2,1,3456,384]{3,2,1,0:T(8,128)(2,1)} %get-tuple-element.387), kind=kLoop, calls=%fused_computation.87.clone.1 | loop fusion | bytes 10616832 | tf_op jit(solution)/shard_map/while/body/eval_jaxpr/slice | solution.py:130
  114.7 2.3 fusion.79
  118.4 4.6 %copy.46 = bf16[3456,384]{1,0:T(8,128)(2,1)} copy(bf16[3456,384]{0,1:T(8,128)(2,1)} %fusion.79) | data formatting | bytes 5308416 | tf_op jit(solution)/shard_map/while/body/eval_jaxpr/convert_element_type | solution.py:59
  123.0 2.7 convolution_bitcast_fusion.5
  125.7 2.8 copy.45
  128.5 2.7 convolution_bitcast_fusion.4
  132.8 3.2 %fusion.75 = (bf16[1,1,3456,384]{3,2,1,0:T(8,128)(2,1)S(1)}, bf16[1,1,3456,384]{3,2,1,0:T(8,128)(2,1)S(1)}) fusion(bf16[2,1,3456,384]{3,2,1,0:T(8,128)(2,1)} %get-tuple-element.387), kind=kLoop, calls=%fused_computation.87.clone.1 | loop fusion | bytes 10616832 | tf_op jit(solution)/shard_map/while/body/eval_jaxpr/slice | solution.py:130
  142.1 2.3 fusion.79
  145.7 4.6 %copy.46 = bf16[3456,384]{1,0:T(8,128)(2,1)} copy(bf16[3456,384]{0,1:T(8,128)(2,1)} %fusion.79) | data formatting | bytes 5308416 | tf_op jit(solution)/shard_map/while/body/eval_jaxpr/convert_element_type | solution.py:59
  150.3 2.7 convolution_bitcast_fusion.5
  153.0 2.8 copy.45
  155.8 2.7 convolution_bitcast_fusion.4
  160.2 3.2 %fusion.75 = (bf16[1,1,3456,384]{3,2,1,0:T(8,128)(2,1)S(1)}, bf16[1,1,3456,384]{3,2,1,0:T(8,128)(2,1)S(1)}) fusion(bf16[2,1,3456,384]{3,2,1,0:T(8,128)(2,1)} %get-tuple-element.387), kind=kLoop, calls=%fused_computation.87.clone.1 | loop fusion | bytes 10616832 | tf_op jit(solution)/shard_map/while/body/eval_jaxpr/slice | solution.py:130
  169.4 2.3 fusion.79
  173.1 4.6 %copy.46 = bf16[3456,384]{1,0:T(8,128)(2,1)} copy(bf16[3456,384]{0,1:T(8,128)(2,1)} %fusion.79) | data formatting | bytes 5308416 | tf_op jit(solution)/shard_map/while/body/eval_jaxpr/convert_element_type | solution.py:59
  177.6 2.7 convolution_bitcast_fusion.5
  180.3 2.8 copy.45
  183.1 2.7 convolution_bitcast_fusion.4
  187.5 3.2 %fusion.75 = (bf16[1,1,3456,384]{3,2,1,0:T(8,128)(2,1)S(1)}, bf16[1,1,3456,384]{3,2,1,0:T(8,128)(2,1)S(1)}) fusion(bf16[2,1,3456,384]{3,2,1,0:T(8,128)(2,1)} %get-tuple-element.387), kind=kLoop, calls=%fused_computation.87.clone.1 | loop fusion | bytes 10616832 | tf_op jit(solution)/shard_map/while/body/eval_jaxpr/slice | solution.py:130
  195.1 1.7 fusion.77
  196.8 2.3 fusion.79
  200.5 4.6 %copy.46 = bf16[3456,384]{1,0:T(8,128)(2,1)} copy(bf16[3456,384]{0,1:T(8,128)(2,1)} %fusion.79) | data formatting | bytes 5308416 | tf_op jit(solution)/shard_map/while/body/eval_jaxpr/convert_element_type | solution.py:59
  205.0 2.7 convolution_bitcast_fusion.5
  207.7 2.8 copy.45
  210.5 2.7 convolution_bitcast_fusion.4
  215.0 3.2 %fusion.75 = (bf16[1,1,3456,384]{3,2,1,0:T(8,128)(2,1)S(1)}, bf16[1,1,3456,384]{3,2,1,0:T(8,128)(2,1)S(1)}) fusion(bf16[2,1,3456,384]{3,2,1,0:T(8,128)(2,1)} %get-tuple-element.387), kind=kLoop, calls=%fused_computation.87.clone.1 | loop fusion | bytes 10616832 | tf_op jit(solution)/shard_map/while/body/eval_jaxpr/slice | solution.py:130
  222.5 1.7 fusion.77
  224.2 2.3 fusion.79
  227.9 4.6 %copy.46 = bf16[3456,384]{1,0:T(8,128)(2,1)} copy(bf16[3456,384]{0,1:T(8,128)(2,1)} %fusion.79) | data formatting | bytes 5308416 | tf_op jit(solution)/shard_map/while/body/eval_jaxpr/convert_element_type | solution.py:59
  232.5 2.7 convolution_bitcast_fusion.5
  235.1 2.8 copy.45
  237.9 2.7 convolution_bitcast_fusion.4
  242.2 5.1 %convert.19 = bf16[2,3,3,384,384]{3,4,2,0,1:T(8,128)(2,1)S(1)} convert(f32[2,3,3,384,384]{3,4,2,0,1:T(8,128)} %get-tuple-element.230) | non-fusion elementwise | flops 2654208 | bytes 15925248 | tf_op jit(solution)/shard_map/convert.8
  247.7 1.9 collective-permute-start.4
  249.7 5.5 %collective-permute-start.5 = (bf16[2,3,384,384]{2,3,1,0:T(8,128)(2,1)S(1)}, bf16[2,3,384,384]{2,3,1,0:T(8,128)(2,1)S(1)}, u32[]{:S(2)}, u32[]{:S(2)}) collective-permute-start(bf16[2,3,384,384]{2,3,1,0:T(8,128)(2,1)S(1)} %get-tuple-element.286), channel_id=1, source_target_pairs={{8,0},{16,8},{24,16},{32,24},{40,32},{48,40},{56,48},{64,56},{72,6... | collective-permute-start | bytes 5308424 | tf_op jit(solution)/shard_map/ppermute | solution.py:16
  255.1 18.0 %collective-permute-done.4 = bf16[2,3,384,384]{2,3,1,0:T(8,128)(2,1)S(1)} collective-permute-done((bf16[2,3,384,384]{2,3,1,0:T(8,128)(2,1)S(1)}, bf16[2,3,384,384]{2,3,1,0:T(8,128)(2,1)S(1)}, u32[]{:S(2)}, u32[]{:S(2)}) %collective-permute-start.4) | collective-permute-done | bytes 1769504 | tf_op jit(solution)/shard_map/ppermute | solution.py:16
  274.6 2.7 fusion.46
  278.5 3.9 %collective-permute-start.6 = (bf16[2,1,384,384]{2,3,0,1:T(8,128)(2,1)}, bf16[2,1,384,384]{2,3,0,1:T(8,128)(2,1)}, u32[]{:S(2)}, u32[]{:S(2)}) collective-permute-start(bf16[2,1,384,384]{2,3,0,1:T(8,128)(2,1)} %get-tuple-element.287), channel_id=1, source_target_pairs={{0,2},{2,4},{4,6},{1,3},{3,5},{5,7},{8,10},{10,12},{12,14},{9,11},... | collective-permute-start | bytes 1769480 | tf_op jit(solution)/shard_map/ppermute | solution.py:16
  282.4 1.9 collective-permute-start.7
  284.4 1.8 copy.31
  286.2 1.8 copy.32
  289.5 5.9 %collective-permute-done.7 = bf16[2,1,384,384]{2,3,0,1:T(8,128)(2,1)} collective-permute-done((bf16[2,1,384,384]{2,3,0,1:T(8,128)(2,1)}, bf16[2,1,384,384]{2,3,0,1:T(8,128)(2,1)}, u32[]{:S(2)}, u32[]{:S(2)}) %collective-permute-start.7) | collective-permute-done | bytes 589856 | tf_op jit(solution)/shard_map/ppermute | solution.py:16
  (191 shorter events, 65.2 us)
Async XLA Ops:
  0.6 37.0 %copy-start.12 = (bf16[6,8,8,384]{3,2,1,0:T(8,128)(2,1)S(1)}, bf16[6,8,8,384]{3,2,1,0:T(8,128)(2,1)}, u32[]{:S(2)}) copy-start(bf16[6,8,8,384]{3,2,1,0:T(8,128)(2,1)} %param.11) | copy-start | bytes 884740
  0.6 37.2 %copy-start.13 = (bf16[6,8,8,384]{3,2,1,0:T(8,128)(2,1)S(1)}, bf16[6,8,8,384]{3,2,1,0:T(8,128)(2,1)}, u32[]{:S(2)}) copy-start(bf16[6,8,8,384]{3,2,1,0:T(8,128)(2,1)} %param.14) | copy-start | bytes 884740
  1.8 19.7 %collective-permute-start.1 = (bf16[2,1,1,384,384]{4,3,2,0,1:T(8,128)(2,1)S(1)}, bf16[2,1,1,384,384]{4,3,2,0,1:T(8,128)(2,1)S(1)}, u32[]{:S(2)}, u32[]{:S(2)}) collective-permute-start(bf16[2,1,1,384,384]{4,3,2,0,1:T(8,128)(2,1)S(1)} %maximum_bitcast_fusion), channel_id=1, source_target_pairs={{8,0},{16,8},{24,16},{32,24},{40,32},{48,40},{56,48},{64,56},{72,6... | collective-permute-start | bytes 1769480 | tf_op jit(solution)/shard_map/ppermute | solution.py:27
  9.6 17.9 %collective-permute-start = (bf16[2,1,1,384,384]{4,3,2,0,1:T(8,128)(2,1)S(1)}, bf16[2,1,1,384,384]{4,3,2,0,1:T(8,128)(2,1)S(1)}, u32[]{:S(2)}, u32[]{:S(2)}) collective-permute-start(bf16[2,1,1,384,384]{4,3,2,0,1:T(8,128)(2,1)S(1)} %maximum_bitcast_fusion), channel_id=1, source_target_pairs={{0,8},{8,16},{16,24},{24,32},{32,40},{40,48},{48,56},{56,64},{64,7... | collective-permute-start | bytes 1769480 | tf_op jit(solution)/shard_map/ppermute | solution.py:24
  28.9 36.3 %copy-start.10 = (bf16[6,8,8,384]{3,2,1,0:T(8,128)(2,1)S(1)}, bf16[6,8,8,384]{3,2,1,0:T(8,128)(2,1)}, u32[]{:S(2)}) copy-start(bf16[6,8,8,384]{3,2,1,0:T(8,128)(2,1)} %param.13) | copy-start | bytes 884740
  28.9 36.3 %copy-start.11 = (bf16[6,8,8,384]{3,2,1,0:T(8,128)(2,1)S(1)}, bf16[6,8,8,384]{3,2,1,0:T(8,128)(2,1)}, u32[]{:S(2)}) copy-start(bf16[6,8,8,384]{3,2,1,0:T(8,128)(2,1)} %param.12) | copy-start | bytes 884740
  28.9 26.5 %collective-permute-start.2 = (bf16[2,3,1,384,384]{4,3,2,0,1:T(8,128)(2,1)}, bf16[2,3,1,384,384]{4,3,2,0,1:T(8,128)(2,1)}, u32[]{:S(2)}, u32[]{:S(2)}) collective-permute-start(bf16[2,3,1,384,384]{4,3,2,0,1:T(8,128)(2,1)} %pad_maximum_fusion.1), channel_id=1, source_target_pairs={{0,2},{2,4},{4,6},{1,3},{3,5},{5,7},{8,10},{10,12},{12,14},{9,11},... | collective-permute-start | bytes 5308424 | tf_op jit(solution)/shard_map/ppermute | solution.py:24
  35.6 25.7 %collective-permute-start.3 = (bf16[2,3,1,384,384]{4,3,2,0,1:T(8,128)(2,1)}, bf16[2,3,1,384,384]{4,3,2,0,1:T(8,128)(2,1)}, u32[]{:S(2)}, u32[]{:S(2)}) collective-permute-start(bf16[2,3,1,384,384]{4,3,2,0,1:T(8,128)(2,1)} %pad_maximum_fusion.1), channel_id=1, source_target_pairs={{2,0},{4,2},{6,4},{3,1},{5,3},{7,5},{10,8},{12,10},{14,12},{11,9},... | collective-permute-start | bytes 5308424 | tf_op jit(solution)/shard_map/ppermute | solution.py:27
  78.1 3.3 %copy-start.2 = (bf16[1,384,384]{1,2,0:T(8,128)(2,1)}, bf16[1,384,384]{1,2,0:T(8,128)(2,1)S(1)}, u32[]{:S(2)}) copy-start(bf16[1,384,384]{1,2,0:T(8,128)(2,1)S(1)} %get-tuple-element.386) | copy-start | bytes 884740 | tf_op jit(solution)/shard_map/while
  78.1 7.7 %copy-start = (bf16[1,384,384]{1,2,0:T(8,128)(2,1)}, bf16[1,384,384]{1,2,0:T(8,128)(2,1)S(1)}, u32[]{:S(2)}) copy-start(bf16[1,384,384]{1,2,0:T(8,128)(2,1)S(1)} %get-tuple-element.388) | copy-start | bytes 884740 | tf_op jit(solution)/shard_map/while
  85.0 0.7 copy-start.7
  91.1 4.6 %copy-start.4 = (bf16[1,384,384]{1,2,0:T(8,128)(2,1)}, bf16[1,384,384]{1,2,0:T(8,128)(2,1)S(1)}, u32[]{:S(2)}) copy-start(bf16[1,384,384]{1,2,0:T(8,128)(2,1)S(1)} %fusion.78) | copy-start | bytes 884740 | tf_op jit(solution)/shard_map/while
  103.8 1.5 copy-start.3
  103.8 1.5 copy-start.8
  104.0 1.3 copy-start.1
  104.0 1.3 copy-start.5
  105.4 3.3 %copy-start.2 = (bf16[1,384,384]{1,2,0:T(8,128)(2,1)}, bf16[1,384,384]{1,2,0:T(8,128)(2,1)S(1)}, u32[]{:S(2)}) copy-start(bf16[1,384,384]{1,2,0:T(8,128)(2,1)S(1)} %get-tuple-element.386) | copy-start | bytes 884740 | tf_op jit(solution)/shard_map/while
  105.4 7.7 %copy-start = (bf16[1,384,384]{1,2,0:T(8,128)(2,1)}, bf16[1,384,384]{1,2,0:T(8,128)(2,1)S(1)}, u32[]{:S(2)}) copy-start(bf16[1,384,384]{1,2,0:T(8,128)(2,1)S(1)} %get-tuple-element.388) | copy-start | bytes 884740 | tf_op jit(solution)/shard_map/while
  112.3 0.7 copy-start.7
  118.4 4.6 %copy-start.4 = (bf16[1,384,384]{1,2,0:T(8,128)(2,1)}, bf16[1,384,384]{1,2,0:T(8,128)(2,1)S(1)}, u32[]{:S(2)}) copy-start(bf16[1,384,384]{1,2,0:T(8,128)(2,1)S(1)} %fusion.78) | copy-start | bytes 884740 | tf_op jit(solution)/shard_map/while
  131.1 1.6 copy-start.3
  131.1 1.6 copy-start.8
  131.3 1.4 copy-start.1
  131.3 1.4 copy-start.5
  132.7 3.3 %copy-start.2 = (bf16[1,384,384]{1,2,0:T(8,128)(2,1)}, bf16[1,384,384]{1,2,0:T(8,128)(2,1)S(1)}, u32[]{:S(2)}) copy-start(bf16[1,384,384]{1,2,0:T(8,128)(2,1)S(1)} %get-tuple-element.386) | copy-start | bytes 884740 | tf_op jit(solution)/shard_map/while
  132.7 7.7 %copy-start = (bf16[1,384,384]{1,2,0:T(8,128)(2,1)}, bf16[1,384,384]{1,2,0:T(8,128)(2,1)S(1)}, u32[]{:S(2)}) copy-start(bf16[1,384,384]{1,2,0:T(8,128)(2,1)S(1)} %get-tuple-element.388) | copy-start | bytes 884740 | tf_op jit(solution)/shard_map/while
  139.6 0.7 copy-start.7
  145.7 4.6 %copy-start.4 = (bf16[1,384,384]{1,2,0:T(8,128)(2,1)}, bf16[1,384,384]{1,2,0:T(8,128)(2,1)S(1)}, u32[]{:S(2)}) copy-start(bf16[1,384,384]{1,2,0:T(8,128)(2,1)S(1)} %fusion.78) | copy-start | bytes 884740 | tf_op jit(solution)/shard_map/while
  158.5 1.5 copy-start.3
  158.5 1.5 copy-start.8
  158.7 1.4 copy-start.1
  158.7 1.4 copy-start.5
  160.0 3.3 %copy-start.2 = (bf16[1,384,384]{1,2,0:T(8,128)(2,1)}, bf16[1,384,384]{1,2,0:T(8,128)(2,1)S(1)}, u32[]{:S(2)}) copy-start(bf16[1,384,384]{1,2,0:T(8,128)(2,1)S(1)} %get-tuple-element.386) | copy-start | bytes 884740 | tf_op jit(solution)/shard_map/while
  160.1 7.7 %copy-start = (bf16[1,384,384]{1,2,0:T(8,128)(2,1)}, bf16[1,384,384]{1,2,0:T(8,128)(2,1)S(1)}, u32[]{:S(2)}) copy-start(bf16[1,384,384]{1,2,0:T(8,128)(2,1)S(1)} %get-tuple-element.388) | copy-start | bytes 884740 | tf_op jit(solution)/shard_map/while
  167.0 0.7 copy-start.7
  173.1 4.6 %copy-start.4 = (bf16[1,384,384]{1,2,0:T(8,128)(2,1)}, bf16[1,384,384]{1,2,0:T(8,128)(2,1)S(1)}, u32[]{:S(2)}) copy-start(bf16[1,384,384]{1,2,0:T(8,128)(2,1)S(1)} %fusion.78) | copy-start | bytes 884740 | tf_op jit(solution)/shard_map/while
  185.8 1.6 copy-start.3
  185.8 1.6 copy-start.8
  186.0 1.4 copy-start.1
  186.0 1.4 copy-start.5
  187.4 3.3 %copy-start.2 = (bf16[1,384,384]{1,2,0:T(8,128)(2,1)}, bf16[1,384,384]{1,2,0:T(8,128)(2,1)S(1)}, u32[]{:S(2)}) copy-start(bf16[1,384,384]{1,2,0:T(8,128)(2,1)S(1)} %get-tuple-element.386) | copy-start | bytes 884740 | tf_op jit(solution)/shard_map/while
  187.4 7.7 %copy-start = (bf16[1,384,384]{1,2,0:T(8,128)(2,1)}, bf16[1,384,384]{1,2,0:T(8,128)(2,1)S(1)}, u32[]{:S(2)}) copy-start(bf16[1,384,384]{1,2,0:T(8,128)(2,1)S(1)} %get-tuple-element.388) | copy-start | bytes 884740 | tf_op jit(solution)/shard_map/while
  194.3 0.7 copy-start.7
  200.4 4.6 %copy-start.4 = (bf16[1,384,384]{1,2,0:T(8,128)(2,1)}, bf16[1,384,384]{1,2,0:T(8,128)(2,1)S(1)}, u32[]{:S(2)}) copy-start(bf16[1,384,384]{1,2,0:T(8,128)(2,1)S(1)} %fusion.78) | copy-start | bytes 884740 | tf_op jit(solution)/shard_map/while
  213.2 1.6 copy-start.3
  213.2 1.6 copy-start.8
  213.4 1.5 copy-start.1
  213.4 1.4 copy-start.5
  214.8 3.3 %copy-start.2 = (bf16[1,384,384]{1,2,0:T(8,128)(2,1)}, bf16[1,384,384]{1,2,0:T(8,128)(2,1)S(1)}, u32[]{:S(2)}) copy-start(bf16[1,384,384]{1,2,0:T(8,128)(2,1)S(1)} %get-tuple-element.386) | copy-start | bytes 884740 | tf_op jit(solution)/shard_map/while
  214.9 7.7 %copy-start = (bf16[1,384,384]{1,2,0:T(8,128)(2,1)}, bf16[1,384,384]{1,2,0:T(8,128)(2,1)S(1)}, u32[]{:S(2)}) copy-start(bf16[1,384,384]{1,2,0:T(8,128)(2,1)S(1)} %get-tuple-element.388) | copy-start | bytes 884740 | tf_op jit(solution)/shard_map/while
  221.8 0.7 copy-start.7
  227.9 4.6 %copy-start.4 = (bf16[1,384,384]{1,2,0:T(8,128)(2,1)}, bf16[1,384,384]{1,2,0:T(8,128)(2,1)S(1)}, u32[]{:S(2)}) copy-start(bf16[1,384,384]{1,2,0:T(8,128)(2,1)S(1)} %fusion.78) | copy-start | bytes 884740 | tf_op jit(solution)/shard_map/while
  240.6 1.6 copy-start.3
  240.6 1.6 copy-start.8
  240.8 1.4 copy-start.1
  240.8 1.4 copy-start.5
  242.2 5.1 %copy-start.6 = (bf16[1,384,384]{1,2,0:T(8,128)(2,1)}, bf16[1,384,384]{1,2,0:T(8,128)(2,1)S(1)}, u32[]{:S(2)}) copy-start(bf16[1,384,384]{1,2,0:T(8,128)(2,1)S(1)} %get-tuple-element.229) | copy-start | bytes 884740
  242.2 5.5 %copy-start.9 = (bf16[1,384,384]{1,2,0:T(8,128)(2,1)}, bf16[1,384,384]{1,2,0:T(8,128)(2,1)S(1)}, u32[]{:S(2)}) copy-start(bf16[1,384,384]{1,2,0:T(8,128)(2,1)S(1)} %get-tuple-element.228) | copy-start | bytes 884740
  247.7 25.4 %collective-permute-start.4 = (bf16[2,3,384,384]{2,3,1,0:T(8,128)(2,1)S(1)}, bf16[2,3,384,384]{2,3,1,0:T(8,128)(2,1)S(1)}, u32[]{:S(2)}, u32[]{:S(2)}) collective-permute-start(bf16[2,3,384,384]{2,3,1,0:T(8,128)(2,1)S(1)} %get-tuple-element.285), channel_id=1, source_target_pairs={{0,8},{8,16},{16,24},{24,32},{32,40},{40,48},{48,56},{56,64},{64,7... | collective-permute-start | bytes 5308424 | tf_op jit(solution)/shard_map/ppermute | solution.py:16
  249.7 24.9 %collective-permute-start.5 = (bf16[2,3,384,384]{2,3,1,0:T(8,128)(2,1)S(1)}, bf16[2,3,384,384]{2,3,1,0:T(8,128)(2,1)S(1)}, u32[]{:S(2)}, u32[]{:S(2)}) collective-permute-start(bf16[2,3,384,384]{2,3,1,0:T(8,128)(2,1)S(1)} %get-tuple-element.286), channel_id=1, source_target_pairs={{8,0},{16,8},{24,16},{32,24},{40,32},{48,40},{56,48},{64,56},{72,6... | collective-permute-start | bytes 5308424 | tf_op jit(solution)/shard_map/ppermute | solution.py:16
  278.5 11.1 %collective-permute-start.6 = (bf16[2,1,384,384]{2,3,0,1:T(8,128)(2,1)}, bf16[2,1,384,384]{2,3,0,1:T(8,128)(2,1)}, u32[]{:S(2)}, u32[]{:S(2)}) collective-permute-start(bf16[2,1,384,384]{2,3,0,1:T(8,128)(2,1)} %get-tuple-element.287), channel_id=1, source_target_pairs={{0,2},{2,4},{4,6},{1,3},{3,5},{5,7},{8,10},{10,12},{12,14},{9,11},... | collective-permute-start | bytes 1769480 | tf_op jit(solution)/shard_map/ppermute | solution.py:16
  282.4 13.0 %collective-permute-start.7 = (bf16[2,1,384,384]{2,3,0,1:T(8,128)(2,1)}, bf16[2,1,384,384]{2,3,0,1:T(8,128)(2,1)}, u32[]{:S(2)}, u32[]{:S(2)}) collective-permute-start(bf16[2,1,384,384]{2,3,0,1:T(8,128)(2,1)} %get-tuple-element.288), channel_id=1, source_target_pairs={{2,0},{4,2},{6,4},{3,1},{5,3},{7,5},{10,8},{12,10},{14,12},{11,9},... | collective-permute-start | bytes 1769480 | tf_op jit(solution)/shard_map/ppermute | solution.py:16
where the time goes:
time: 300 us; the launch traced here: 299 us
  local copies, waits for them, and re-layouts  94.6 us (32%)
  matrix products  66.4 us (22%)
  waiting for transfers between devices  62.1 us (21%)
  other arithmetic  42.4 us (14%)
  starting transfers between devices  31.5 us (10%)
    convert_element_type x6, local copies, waits for them, and re-layouts, query_head(): weights_low = jnp.exp(scores - logsum).astype(jnp.bfloat16)  27.3 us
    ppermute x4, waiting for transfers between devices, passed_along(): return lax.ppermute(array, axis, pairs)  26.8 us
    ppermute x2, waiting for transfers between devices, padded(): lax.ppermute(lax.slice_in_dim(block, block.shape[dim] - width, None, axis...  22.2 us
    slice x6, local copies, waits for them, and re-layouts, forward_step(): neighbours[0]  19.1 us
    convert_element_type x6, local copies, waits for them, and re-layouts, query_head(): (jnp.exp(scores - logsum) * (product - carried[:, :, None]) * scale).asty...  16.8 us
    dot_general x6, matrix products, query_head(): jnp.einsum('tqk,tqd->tkd', weights_low, grad_rows, preferred_element_type...  16.1 us
    dot_general x6, matrix products, query_head(): jnp.einsum('tqk,tqd->tkd', slopes, query_rows, preferred_element_type=jnp...  16.1 us
    convert_element_type x6, other arithmetic, query_head(): weights_low = jnp.exp(scores - logsum).astype(jnp.bfloat16)  14.1 us
  transfers between devices with their start and end apart: 8, of which 8 were waited for; matrix products, arithmetic and copies ran while one was open for 3% of the time, Pallas kernels for 0%

commit v1 on v0

v1 whole, which is shorter than its diff:
```python
import functools

import jax
import jax.numpy as jnp
from jax import lax
from jax.experimental import pallas as pl
from jax.experimental.pallas import tpu as pltpu
from jax.sharding import PartitionSpec as P

MESH = pl.DeviceIdType.MESH
F32 = jnp.float32
BF16 = jnp.bfloat16
DIM = 64
TILE = 384
HEADS = 6
NEAR = 3
FAR = 1e30


def swap_halves(x):
    return pltpu.roll(x, DIM, 1)


def kernel(
    tiles_t,
    mask_ref, q_ref, k_ref, v_ref, g_ref,
    att_ref, qg_ref, kg_ref, vg_ref,
    kv_own, qd_own, kv, qd, dkv, terms, oq, oq_all,
    e_s, eh_s, ds_s, w_s, ot_s, m_s, l_s, qt_s, dqt_s, kvt_s,
    kv_send, kv_recv, qd_send, qd_recv, dkv_send, dkv_recv, oq_send, oq_recv,
):
    t = lax.axis_index("tm")
    h = lax.axis_index("height")
    hi = h // 2
    core = h % 2
    inner = jnp.where(hi == 0, core, 1 - core)
    sibling = 2 * hi + 1 - core
    outer_h, inner_h, partner_h = 3 * hi, 1 + hi, 2 - hi
    heights = (outer_h, inner_h, partner_h)
    has = {-1: t > 0, 0: t >= 0, 1: t < tiles_t - 1}

    barrier = pltpu.get_barrier_semaphore()
    for dt in (-1, 0, 1):
        @pl.when(has[dt])
        def _():
            for dh in range(1 if dt == 0 else 0, 4):
                pl.semaphore_signal(
                    barrier, inc=1, device_id={"tm": t + dt, "height": lax.rem(h + dh, 4)}, device_id_type=MESH
                )

    lane = lax.broadcasted_iota(jnp.int32, (TILE, 2 * DIM), 1)
    low = lane < DIM

    def pack(pair, _):
        cols = pl.ds(pl.multiple_of(pair * 2 * DIM, 2 * DIM), 2 * DIM)
        for own, a_ref, b_ref, factor in ((kv_own, k_ref, v_ref, 1.0), (qd_own, q_ref, g_ref, 0.125)):
            a = a_ref[:, cols].astype(F32) * factor
            b = b_ref[:, cols].astype(F32)
            own[2 * pair] = jnp.where(low, a, swap_halves(b)).astype(BF16)
            own[2 * pair + 1] = jnp.where(low, swap_halves(a), b).astype(BF16)
        return 0

    lax.fori_loop(0, HEADS // 2, pack, 0)
    for dt in (-1, 1):
        @pl.when(jnp.logical_not(has[dt]))
        def _():
            for n in range(NEAR):
                for u in range(3):
                    kv[n, 3 * (dt + 1) + u] = jnp.zeros((TILE, 2 * DIM), BF16)
            for n in range(HEADS):
                terms[n, 1 + dt] = jnp.zeros((TILE, 2 * DIM), BF16)
                terms[n, 4 + dt] = jnp.zeros((TILE, 2 * DIM), BF16)
    for n in range(NEAR):
        kv[n, 3 + inner] = kv_own[3 * core + n]
        qd[n, inner] = qd_own[3 * core + n]
    count = 4 * (1 + (t > 0).astype(jnp.int32) + (t < tiles_t - 1).astype(jnp.int32)) - 1
    pl.semaphore_wait(barrier, count)

    def qd_copy(n):
        return pltpu.make_async_remote_copy(
            src_ref=qd_own.at[3 * (1 - core) + n], dst_ref=qd.at[n, inner],
            send_sem=qd_send.at[n], recv_sem=qd_recv.at[n],
            device_id={"height": sibling}, device_id_type=MESH,
        )

    def kv_copy(n, dt, far, to):
        chip = 1 - hi if far else hi
        slot = 3 * (1 - dt) + (2 if far else inner)
        return pltpu.make_async_remote_copy(
            src_ref=kv_own.at[3 * to + n], dst_ref=kv.at[n, slot],
            send_sem=kv_send.at[n, (dt + 1) * 4 + 2 * far + (0 if isinstance(to, int) and to == 0 else 1)],
            recv_sem=kv_recv.at[n, slot],
            device_id={"tm": t + dt, "height": 2 * chip + to}, device_id_type=MESH,
        )

    def each_kv(n, act, with_centre=True):
        act(kv_copy(n, 0, 0, 1 - core))
        for dt in (-1, 1):
            @pl.when(has[dt])
            def _():
                for to in range(2):
                    act(kv_copy(n, dt, 0, to))
        for dt in (0, -1, 1):
            @pl.when((inner == 1) & has[dt])
            def _():
                for to in range(2):
                    act(kv_copy(n, dt, 1, to))

    def send_head(n, _):
        qd_copy(n).start()
        each_kv(n, lambda c: c.start())
        return 0

    lax.fori_loop(0, NEAR, send_head, 0)

    def wait_kv(n, slot):
        pltpu.make_async_remote_copy(
            src_ref=kv_own.at[0], dst_ref=kv.at[n, slot], send_sem=kv_send.at[0, 0], recv_sem=kv_recv.at[n, slot],
            device_id={"height": sibling}, device_id_type=MESH,
        ).wait_recv()

    def allowed(dt, u):
        def one(query_h, key_h):
            o = 3 * (dt + 1) + key_h - query_h + 1
            flag = mask_ref[(t * 4 + query_h) * 9 + o]
            flag = jnp.where(o == 4, 1, flag)
            return jnp.where(has[dt], flag, 0)

        inner_flag = one(inner_h, heights[u])
        if u == 2:
            return jnp.full((1, TILE), inner_flag, jnp.int32)
        spot = lax.broadcasted_iota(jnp.int32, (1, 2 * TILE), 1)
        return jnp.where(spot < TILE, one(outer_h, heights[u]), inner_flag)

    def slots(group):
        return [3 * group, 3 * group + 1] if group < 3 else [2, 5, 8]

    def keys(n, group):
        if group < 3:
            return kv[n, 3 * group:3 * group + 2].reshape(2 * TILE, 2 * DIM)
        return jnp.concatenate([kv[n, j] for j in slots(3)], 0)

    def forward(n, group):
        js = slots(group)
        first = 0 if group < 3 else TILE
        for j in js:
            kvt_s[n, j] = kv[n, j].astype(F32).T.astype(BF16)
        scores = jnp.dot(keys(n, group), qt_s[n, 0, :, first:], preferred_element_type=F32)
        flags = [allowed(j // 3 - 1, j % 3) > 0 for j in js]
        tops = [
            jnp.where(flag, jnp.max(scores[i * TILE:(i + 1) * TILE], axis=0, keepdims=True), -FAR)
            for i, flag in enumerate(flags)
        ]
        top = functools.reduce(jnp.maximum, tops)
        total = 0.0
        parts = []
        for i, flag in enumerate(flags):
            e = jnp.exp(scores[i * TILE:(i + 1) * TILE] - jnp.where(flag, top, FAR))
            total = total + jnp.sum(e, axis=0, keepdims=True)
            parts.append(e.astype(BF16))
        e = jnp.concatenate(parts, 0)
        if group < 3:
            e_s[n, group] = e
        else:
            eh_s[...] = e
        values = jnp.concatenate([kvt_s[n, j, DIM:] for j in js], 1)
        ot_s[n, group, :, first:] = jnp.dot(values, e, preferred_element_type=F32)
        m_s[n, group:group + 1, first:] = top
        l_s[n, group:group + 1, first:] = total

    def centre(n, _):
        wait_kv(n, 4 - inner)
        qd_copy(n).wait_recv()
        turned = qd[n].reshape(2 * TILE, 2 * DIM).astype(F32).T
        zero = jnp.zeros((DIM, 2 * TILE), BF16)
        qt_s[n, 0] = jnp.concatenate([turned[:DIM].astype(BF16), zero], 0)
        qt_s[n, 1] = jnp.concatenate([zero, turned[DIM:].astype(BF16)], 0)
        forward(n, 1)
        return 0

    lax.fori_loop(0, NEAR, centre, 0)

    def dkv_copy(n, dt, u):
        return pltpu.make_async_remote_copy(
            src_ref=dkv.at[n, 3 * (dt + 1) + u], dst_ref=terms.at[3 * core + n, (4 if u == 2 else 1) - dt],
            send_sem=dkv_send.at[n, 3 * (dt + 1) + u], recv_sem=dkv_recv.at[3 * core + n, (4 if u == 2 else 1) - dt],
            device_id={"tm": t + dt, "height": heights[u]}, device_id_type=MESH,
        )

    def dkv_near_copy(n):
        return pltpu.make_async_remote_copy(
            src_ref=dkv.at[n, 4 - inner], dst_ref=terms.at[3 * core + n, 1],
            send_sem=dkv_send.at[n, 4], recv_sem=dkv_recv.at[3 * core + n, 1],
            device_id={"height": sibling}, device_id_type=MESH,
        )

    def oq_copy(n):
        return pltpu.make_async_remote_copy(
            src_ref=oq.at[n, 1 - inner], dst_ref=oq_all.at[3 * core + n],
            send_sem=oq_send.at[n], recv_sem=oq_recv.at[n],
            device_id={"height": sibling}, device_id_type=MESH,
        )

    def head(n, _):
        for dt in (-1, 1):
            @pl.when(has[dt])
            def _():
                wait_kv(n, 3 * (dt + 1))
                wait_kv(n, 3 * (dt + 1) + 1)
            forward(n, dt + 1)
        for dt in (-1, 0, 1):
            @pl.when(has[dt])
            def _():
                wait_kv(n, 3 * (dt + 1) + 2)
        forward(n, 3)
        m_s[n, 3:4, :TILE] = jnp.full((1, TILE), -FAR, F32)
        l_s[n, 3:4, :TILE] = jnp.zeros((1, TILE), F32)
        tops = m_s[n, 0:4]
        shares = jnp.exp(tops - jnp.max(tops, axis=0, keepdims=True))
        shares = shares / jnp.sum(shares * l_s[n, 0:4], axis=0, keepdims=True)
        out = ot_s[n, 0] * shares[0:1] + ot_s[n, 1] * shares[1:2] + ot_s[n, 2] * shares[2:3]
        out = jnp.concatenate([out[:, :TILE], out[:, TILE:] + ot_s[n, 3, :, TILE:] * shares[3:4, TILE:]], 1)
        out = out.astype(BF16).astype(F32)
        carried = jnp.sum(qt_s[n, 1, DIM:].astype(F32) * out, axis=0, keepdims=True)

        def backward(group):
            first = 0 if group < 3 else TILE
            size = 768 if group < 3 else 1152
            js = slots(group)
            product = jnp.dot(keys(n, group), qt_s[n, 1, :, first:], preferred_element_type=F32)
            e = e_s[n, group] if group < 3 else eh_s[...]
            weights = e.astype(F32) * shares[group:group + 1, first:]
            slopes = (weights * (product - carried[:, first:])).astype(BF16)
            ds_s[:size, first:] = slopes
            w_s[:size, first:] = weights.astype(BF16)
            turned = jnp.concatenate([kvt_s[n, j, :DIM] for j in js], 1)
            part = jnp.dot(turned, slopes, preferred_element_type=F32)
            if group == 0:
                dqt_s[...] = part
            else:
                dqt_s[:, first:] += part
            rhs = qd[n].reshape(2 * TILE, 2 * DIM)[first:]
            key_part = jnp.dot(ds_s[:size, first:], rhs, preferred_element_type=F32)
            value_part = jnp.dot(w_s[:size, first:], rhs, preferred_element_type=F32)
            lanes = lax.broadcasted_iota(jnp.int32, (size, 2 * DIM), 1)
            both = jnp.where(lanes < DIM, key_part, value_part).astype(BF16)
            for i, j in enumerate(js):
                dkv[n, j] = both[i * TILE:(i + 1) * TILE]

        for dt in (-1, 1):
            backward(dt + 1)
            @pl.when(has[dt])
            def _():
                for u in range(2):
                    dkv_copy(n, dt, u).start()
        backward(3)
        for dt in (-1, 0, 1):
            @pl.when(has[dt])
            def _():
                dkv_copy(n, dt, 2).start()
        backward(1)
        dkv_near_copy(n).start()
        terms[3 * core + n, 1] = dkv[n, 3 + inner]
        both = jnp.concatenate([out, dqt_s[...] * 0.125], 0).T.astype(BF16)
        oq[n, 0] = both[:TILE]
        oq[n, 1] = both[TILE:]
        oq_copy(n).start()
        oq_all[3 * core + n] = oq[n, inner]
        return 0

    lax.fori_loop(0, NEAR, head, 0)

    def wait_term(n, term):
        pltpu.make_async_remote_copy(
            src_ref=dkv.at[0, 0], dst_ref=terms.at[n, term], send_sem=dkv_send.at[0, 0], recv_sem=dkv_recv.at[n, term],
            device_id={"height": sibling}, device_id_type=MESH,
        ).wait_recv()

    for n in range(NEAR):
        pltpu.make_async_remote_copy(
            src_ref=oq.at[n, 0], dst_ref=oq_all.at[3 * (1 - core) + n], send_sem=oq_send.at[n], recv_sem=oq_recv.at[n],
            device_id={"height": sibling}, device_id_type=MESH,
        ).wait_recv()
        wait_term(3 * (1 - core) + n, 1)
        for c in range(2):
            for dt in (-1, 1):
                @pl.when(has[dt])
                def _():
                    wait_term(3 * c + n, 1 + dt)
            for dt in (-1, 0, 1):
                @pl.when(has[dt] & (inner == 1))
                def _():
                    wait_term(3 * c + n, 4 + dt)

    def finish(pair, _):
        cols = pl.ds(pl.multiple_of(pair * 2 * DIM, 2 * DIM), 2 * DIM)

        def store(even, odd, a_ref, b_ref):
            a_ref[:, cols] = jnp.where(low, even, swap_halves(odd)).astype(BF16)
            b_ref[:, cols] = jnp.where(low, swap_halves(even), odd).astype(BF16)

        store(oq_all[2 * pair].astype(F32), oq_all[2 * pair + 1].astype(F32), att_ref, qg_ref)

        def summed(n, count):
            total = terms[n, 0].astype(F32)
            for i in range(1, count):
                total = total + terms[n, i].astype(F32)
            return total

        @pl.when(inner == 1)
        def _():
            store(summed(2 * pair, 6), summed(2 * pair + 1, 6), kg_ref, vg_ref)

        @pl.when(inner == 0)
        def _():
            store(summed(2 * pair, 3), summed(2 * pair + 1, 3), kg_ref, vg_ref)

        return 0

    lax.fori_loop(0, HEADS // 2, finish, 0)

    def drain(n, _):
        qd_copy(n).wait_send()
        each_kv(n, lambda c: c.wait_send())
        for dt in (-1, 1):
            @pl.when(has[dt])
            def _():
                for u in range(2):
                    dkv_copy(n, dt, u).wait_send()
        for dt in (-1, 0, 1):
            @pl.when(has[dt])
            def _():
                dkv_copy(n, dt, 2).wait_send()
        dkv_near_copy(n).wait_send()
        oq_copy(n).wait_send()
        return 0

    lax.fori_loop(0, NEAR, drain, 0)


def local(tiles_t, queries, key_tokens, value_tokens, cotangent, window_mask):
    flat = (TILE, HEADS * DIM)
    vmem = pl.BlockSpec(memory_space=pltpu.VMEM)
    block = (TILE, 2 * DIM)
    dma = pltpu.SemaphoreType.DMA
    outs = pl.pallas_call(
        functools.partial(kernel, tiles_t),
        out_shape=[jax.ShapeDtypeStruct(flat, BF16)] * 4,
        in_specs=[pl.BlockSpec(memory_space=pltpu.SMEM)] + [vmem] * 4,
        out_specs=[vmem] * 4,
        scratch_shapes=[
            pltpu.VMEM((HEADS, *block), BF16),
            pltpu.VMEM((HEADS, *block), BF16),
            pltpu.VMEM((NEAR, 9, *block), BF16),
            pltpu.VMEM((NEAR, 2, *block), BF16),
            pltpu.VMEM((NEAR, 9, *block), BF16),
            pltpu.VMEM((HEADS, 6, *block), BF16),
            pltpu.VMEM((NEAR, 2, *block), BF16),
            pltpu.VMEM((HEADS, *block), BF16),
            pltpu.VMEM((NEAR, 3, 768, 768), BF16),
            pltpu.VMEM((1152, 384), BF16),
            pltpu.VMEM((1152, 768), BF16),
            pltpu.VMEM((1152, 768), BF16),
            pltpu.VMEM((NEAR, 4, DIM, 768), F32),
            pltpu.VMEM((NEAR, 8, 768), F32),
            pltpu.VMEM((NEAR, 8, 768), F32),
            pltpu.VMEM((NEAR, 2, 2 * DIM, 768), BF16),
            pltpu.VMEM((DIM, 768), F32),
            pltpu.VMEM((NEAR, 9, 2 * DIM, TILE), BF16),
            dma((NEAR, 12)),
            dma((NEAR, 9)),
            dma((NEAR,)),
            dma((NEAR,)),
            dma((NEAR, 9)),
            dma((HEADS, 6)),
            dma((NEAR,)),
            dma((NEAR,)),
        ],
        compiler_params=pltpu.CompilerParams(
            collective_id=0, has_side_effects=True, vmem_limit_bytes=60 * 1024 * 1024
        ),
    )(
        window_mask.reshape(-1),
        queries.reshape(flat), key_tokens.reshape(flat), value_tokens.reshape(flat), cotangent.reshape(flat),
    )
    return tuple(out.reshape(queries.shape) for out in outs)


def solution(mesh):
    spec = P("tm", "height", None, "heads")
    return jax.shard_map(
        functools.partial(local, mesh.shape["tm"]), mesh=mesh, in_specs=(spec,) * 4 + (P(),), out_specs=(spec,) * 4,
        check_vma=False,
    )
```

time: 300 us -> 63.3 us (0.21)
  local copies, waits for them, and re-layouts: 94.6 us -> 6.24 us
  matrix products: 66.4 us -> 0 us
  waiting for transfers between devices: 62.1 us -> 0 us
  Pallas kernels: 0 us -> 56.2 us
  other arithmetic: 42.4 us -> 0 us
  starting transfers between devices: 31.5 us -> 0 us
    dot_general x36 -> x0, matrix products: 66.4 us -> none  [the longest x6 16.1 us: query_head(): jnp.einsum('tqk,tqd->tkd', weights_low, grad_rows, preferred_element_type...]
    ppermute x8 -> x0, waiting for transfers between devices: 62.1 us -> none  [the longest x4 26.8 us: passed_along(): return lax.ppermute(array, axis, pairs)]
    pallas_call x0 -> x1, Pallas kernels: none -> 56.2 us  [local(): pl.pallas_call(functools.partial(kernel, tiles_t), out_shape=[jax.ShapeDt...]
    convert_element_type x14 -> x0, local copies, waits for them, and re-layouts: 45.7 us -> none  [the longest x6 27.3 us: query_head(): weights_low = jnp.exp(scores - logsum).astype(jnp.bfloat16)]
    ppermute x8 -> x0, starting transfers between devices: 31.5 us -> none  [the longest x4 13.3 us: passed_along(): return lax.ppermute(array, axis, pairs)]
    slice x9 -> x0, local copies, waits for them, and re-layouts: 20.9 us -> none  [the longest x6 19.1 us: forward_step(): neighbours[0]]
    convert_element_type x6 -> x0, other arithmetic: 14.1 us -> none  [query_head(): weights_low = jnp.exp(scores - logsum).astype(jnp.bfloat16)]
    another operation x3 -> x0, other arithmetic: 9.19 us -> none
  transfers between devices with their start and end apart: 8 -> 0, of which waited for: 8 -> 0; matrix products, arithmetic and copies ran while one was open for 3% -> 0% of each run, Pallas kernels for 0% -> 0%
where the time goes in v1:
time: 63.3 us; the launch traced here: 63.1 us
  Pallas kernels  56.2 us (89%)
  local copies, waits for them, and re-layouts  6.24 us (10%)
  between operations  0.65 us (1%)
    pallas_call x1, Pallas kernels, local(): pl.pallas_call(functools.partial(kernel, tiles_t), out_shape=[jax.ShapeDt...  56.2 us
    unnamed x11, local copies, waits for them, and re-layouts  5.43 us

profile of v1, /device:TPU:7, one launch (start us, length us, event | category | flops | bytes accessed | tf_op | source)
XLA Modules:
  0.0 63.1 jit_solution(7697050657242111948)
XLA Ops:
  0.6 0.8 %copy.9 = s32[32,4,9]{2,1,0:T(4,128)S(1)} copy(s32[32,4,9]{0,1,2:T(4,128)} %param.9) | data formatting | bytes 9216 | tf_op args[4]
  1.5 0.8 %reshape.35.mask_ref = s32[1152]{0:T(1024)} reshape(s32[32,4,9]{2,1,0:T(4,128)S(1)} %copy.9) | data formatting | bytes 9216 | tf_op jit(solution)/shard_map/reshape | solution.py:383
  2.3 56.2 %shard_map.84 = (bf16[384,384]{1,0:T(8,128)(2,1)}, bf16[384,384]{1,0:T(8,128)(2,1)}, bf16[384,384]{1,0:T(8,128)(2,1)}, bf16[384,384]{1,0:T(8,128)(2,1)}) custom-call(s32[1152]{0:T(1024)} %reshape.35.mask_ref, bf16[384,384]{1,0:T(8,128)(2,1)} %bitcast.12, bf16[384,384]{1,0:T(8,128)(2,1)} %bitcast.13, bf16[384,384]{1,0:T(8,128)(2,1)} %bitcast.14, ...), custom_call_target="tpu_custom_call" | custom-call | tf_op jit(solution)/shard_map/pallas_call | solution.py:346
  58.4 0.0 copy-start.2
  58.5 1.7 %copy.14 = bf16[6,8,8,384]{3,2,1,0:T(8,128)(2,1)} copy(bf16[6,8,8,384]{3,2,1,0:T(8,128)(2,1)} %bitcast.11) | data formatting | bytes 589824
  60.2 0.0 copy-done.2
  60.2 0.0 copy-start.1
  60.2 0.7 %copy.15 = bf16[6,8,8,384]{3,2,1,0:T(8,128)(2,1)} copy(bf16[6,8,8,384]{3,2,1,0:T(8,128)(2,1)S(1)} %bitcast.10) | data formatting | bytes 589824
  60.9 0.4 copy-done.1
  61.3 0.0 copy-start
  61.3 0.7 %copy.16 = bf16[6,8,8,384]{3,2,1,0:T(8,128)(2,1)} copy(bf16[6,8,8,384]{3,2,1,0:T(8,128)(2,1)S(1)} %bitcast.9) | data formatting | bytes 589824
  62.0 0.4 copy-done
  62.3 0.7 %copy.17 = bf16[6,8,8,384]{3,2,1,0:T(8,128)(2,1)} copy(bf16[6,8,8,384]{3,2,1,0:T(8,128)(2,1)S(1)} %bitcast.8) | data formatting | bytes 589824
Async XLA Ops:
  58.4 1.8 %copy-start.2 = (bf16[384,384]{1,0:T(8,128)(2,1)S(1)}, bf16[384,384]{1,0:T(8,128)(2,1)}, u32[]{:S(2)}) copy-start(bf16[384,384]{1,0:T(8,128)(2,1)} %get-tuple-element.9) | copy-start | bytes 884740
  60.2 1.1 %copy-start.1 = (bf16[384,384]{1,0:T(8,128)(2,1)S(1)}, bf16[384,384]{1,0:T(8,128)(2,1)}, u32[]{:S(2)}) copy-start(bf16[384,384]{1,0:T(8,128)(2,1)} %get-tuple-element.10) | copy-start | bytes 884740
  61.3 1.1 %copy-start = (bf16[384,384]{1,0:T(8,128)(2,1)S(1)}, bf16[384,384]{1,0:T(8,128)(2,1)}, u32[]{:S(2)}) copy-start(bf16[384,384]{1,0:T(8,128)(2,1)} %get-tuple-element.11) | copy-start | bytes 884740

commit v2 on v1

v2 whole, which is shorter than its diff:
```python
import functools

import jax
import jax.numpy as jnp
from jax import lax
from jax.experimental import pallas as pl
from jax.experimental.pallas import tpu as pltpu
from jax.sharding import PartitionSpec as P

MESH = pl.DeviceIdType.MESH
F32 = jnp.float32
BF16 = jnp.bfloat16
DIM = 64
TILE = 384
HEADS = 6
NEAR = 3
FAR = 1e30


def swap_halves(x):
    return pltpu.roll(x, DIM, 1)


def kernel(
    tiles_t,
    mask_hbm, q_hbm, k_hbm, v_hbm, g_hbm,
    att_ref, qg_ref, kg_ref, vg_ref,
    arrays, mask_s, flag_s, kv_own, qd_own, kv, qd, dkv, y_back, z_back, terms, oq, oq_all,
    e_s, eh_s, ds_s, w_s, ot_s, m_s, l_s, qt_s, dqt_s, kvt_s,
    load_sem, kv_send, kv_recv, pass_send, qd_send, qd_recv, dkv_send, dkv_recv, y_recv, z_recv, oq_send, oq_recv,
):
    t = lax.axis_index("tm")
    h = lax.axis_index("height")
    hi = h // 2
    core = h % 2
    inner = jnp.where(hi == 0, core, 1 - core)
    sibling = 2 * hi + 1 - core
    outer_h, inner_h, partner_h = 3 * hi, 1 + hi, 2 - hi
    heights = (outer_h, inner_h, partner_h)
    has = {-1: t > 0, 0: t >= 0, 1: t < tiles_t - 1}

    barrier = pltpu.get_barrier_semaphore()
    for dt in (-1, 0, 1):
        @pl.when(has[dt])
        def _():
            for height in (h, sibling) if dt else (sibling, 2 - 2 * hi, 3 - 2 * hi):
                pl.semaphore_signal(barrier, inc=1, device_id={"tm": t + dt, "height": height}, device_id_type=MESH)

    loads = [
        pltpu.make_async_copy(ref, arrays.at[i], load_sem.at[i]) for i, ref in enumerate((k_hbm, v_hbm, q_hbm, g_hbm))
    ] + [pltpu.make_async_copy(mask_hbm, mask_s, load_sem.at[4])]
    for load in loads:
        load.start()

    lane = lax.broadcasted_iota(jnp.int32, (TILE, 2 * DIM), 1)
    low = lane < DIM
    for load in loads[:2]:
        load.wait()

    def pack(own, first, factor, pair, _):
        cols = pl.ds(pl.multiple_of(pair * 2 * DIM, 2 * DIM), 2 * DIM)
        a = arrays[first, :, cols].astype(F32) * factor
        b = arrays[first + 1, :, cols].astype(F32)
        own[2 * pair] = jnp.where(low, a, swap_halves(b)).astype(BF16)
        own[2 * pair + 1] = jnp.where(low, swap_halves(a), b).astype(BF16)
        return 0

    lax.fori_loop(0, HEADS // 2, functools.partial(pack, kv_own, 0, 1.0), 0)
    for load in loads[2:]:
        load.wait()
    lax.fori_loop(0, HEADS // 2, functools.partial(pack, qd_own, 2, 0.125), 0)
    for dt in (-1, 1):
        @pl.when(jnp.logical_not(has[dt]))
        def _():
            for n in range(NEAR):
                for u in range(3):
                    kv[n, 3 * (dt + 1) + u] = jnp.zeros((TILE, 2 * DIM), BF16)
            for n in range(HEADS):
                terms[n, 1 + dt] = jnp.zeros((TILE, 2 * DIM), BF16)
            for n in range(2):
                z_back[n, (1 + dt) // 2] = jnp.zeros((TILE, 2 * DIM), BF16)
    for n in range(NEAR):
        kv[n, 3 + inner] = kv_own[3 * core + n]
        qd[n, inner] = qd_own[3 * core + n]
    spot = lax.broadcasted_iota(jnp.int32, (9, 4, tiles_t), 2)
    row = lax.broadcasted_iota(jnp.int32, (9, 4, tiles_t), 1)
    for i, query_h in enumerate((outer_h, inner_h)):
        chosen = jnp.where((spot == t) & (row == query_h), mask_s[...], 0).astype(F32)
        chosen = jnp.sum(jnp.sum(chosen, axis=2, keepdims=True), axis=1, keepdims=True)
        flag_s[i] = jnp.broadcast_to(chosen, (9, 1, 2 * DIM))

    count = 3 + 2 * ((t > 0).astype(jnp.int32) + (t < tiles_t - 1).astype(jnp.int32))
    pl.semaphore_wait(barrier, count)

    def qd_copy(n):
        return pltpu.make_async_remote_copy(
            src_ref=qd_own.at[3 * (1 - core) + n], dst_ref=qd.at[n, inner],
            send_sem=qd_send.at[n], recv_sem=qd_recv.at[n],
            device_id={"height": sibling}, device_id_type=MESH,
        )

    def kv_copy(n, dt, to, far=0):
        slot = 3 * (1 - dt) + (2 if far else inner)
        index = 5 + to if far else {-1: to, 0: 2, 1: 3 + to}[dt]
        return pltpu.make_async_remote_copy(
            src_ref=kv_own.at[3 * to + n], dst_ref=kv.at[n, slot],
            send_sem=kv_send.at[n, index], recv_sem=kv_recv.at[n, slot],
            device_id={"tm": t + dt, "height": 2 * (1 - hi if far else hi) + to}, device_id_type=MESH,
        )

    def kv_along(n, act):
        for dt in (-1, 1):
            @pl.when(has[dt])
            def _():
                for to in range(2):
                    act(kv_copy(n, dt, to))

    def kv_beside(n, act):
        act(kv_copy(n, 0, 1 - core))

        @pl.when(inner == 1)
        def _():
            for to in range(2):
                act(kv_copy(n, 0, to, 1))

    def pass_over(n, dt):
        slot = 3 * (dt + 1)
        return pltpu.make_async_remote_copy(
            src_ref=kv.at[n, slot + 1], dst_ref=kv.at[n, slot + 2],
            send_sem=pass_send.at[n, (dt + 1) // 2], recv_sem=kv_recv.at[n, slot + 2],
            device_id={"height": 2 * (1 - hi) + core}, device_id_type=MESH,
        )

    def pass_along(n, dt):
        slot = 3 * (1 - dt) + 2
        return pltpu.make_async_remote_copy(
            src_ref=kv.at[n, 5], dst_ref=kv.at[n, slot],
            send_sem=pass_send.at[n, (dt + 1) // 2], recv_sem=kv_recv.at[n, slot],
            device_id={"tm": t + dt}, device_id_type=MESH,
        )

    def send_head(n, _):
        qd_copy(n).start()
        kv_beside(n, lambda c: c.start())

        @pl.when(n < 2)
        def _():
            kv_along(n, lambda c: c.start())
        return 0

    lax.fori_loop(0, NEAR, send_head, 0)

    def wait_kv(n, slot):
        pltpu.make_async_remote_copy(
            src_ref=kv_own.at[0], dst_ref=kv.at[n, slot], send_sem=kv_send.at[0, 0], recv_sem=kv_recv.at[n, slot],
            device_id={"height": sibling}, device_id_type=MESH,
        ).wait_recv()

    def passes_along(n):
        wait_kv(n, 5)
        for dt in (-1, 1):
            @pl.when(has[dt])
            def _():
                pass_along(n, dt).start()

    def allowed(dt, u):
        def one(i, query_h, key_h):
            if dt == 0 and i == u:
                return jnp.ones((1, TILE), F32)
            flag = flag_s[i, 3 * (dt + 1) + key_h - query_h + 1] * has[dt].astype(F32)
            return jnp.concatenate([flag] * 3, 1)

        inner_flag = one(1, inner_h, heights[u])
        if u == 2:
            return inner_flag
        return jnp.concatenate([one(0, outer_h, heights[u]), inner_flag], 1)

    def slots(group):
        return [3 * group, 3 * group + 1] if group < 3 else [2, 5, 8]

    def keys(n, group):
        if group < 3:
            return kv[n, 3 * group:3 * group + 2].reshape(2 * TILE, 2 * DIM)
        return jnp.concatenate([kv[n, j] for j in slots(3)], 0)

    def forward(n, group):
        js = slots(group)
        first = 0 if group < 3 else TILE
        for j in js:
            kvt_s[n, j] = kv[n, j].astype(F32).T.astype(BF16)
        scores = jnp.dot(keys(n, group), qt_s[n, 0, :, first:], preferred_element_type=F32)
        flags = [allowed(j // 3 - 1, j % 3) > 0 for j in js]
        tops = [
            jnp.where(flag, jnp.max(scores[i * TILE:(i + 1) * TILE], axis=0, keepdims=True), -FAR)
            for i, flag in enumerate(flags)
        ]
        top = functools.reduce(jnp.maximum, tops)
        total = 0.0
        parts = []
        for i, flag in enumerate(flags):
            e = jnp.exp(scores[i * TILE:(i + 1) * TILE] - jnp.where(flag, top, FAR))
            total = total + jnp.sum(e, axis=0, keepdims=True)
            parts.append(e.astype(BF16))
        e = jnp.concatenate(parts, 0)
        if group < 3:
            e_s[n, group] = e
        else:
            eh_s[...] = e
        values = jnp.concatenate([kvt_s[n, j, DIM:] for j in js], 1)
        ot_s[n, group, :, first:] = jnp.dot(values, e, preferred_element_type=F32)
        m_s[n, group:group + 1, first:] = top
        l_s[n, group:group + 1, first:] = total

    def centre(n, _):
        wait_kv(n, 4 - inner)
        qd_copy(n).wait_recv()
        turned = qd[n].reshape(2 * TILE, 2 * DIM).astype(F32).T
        zero = jnp.zeros((DIM, 2 * TILE), BF16)
        qt_s[n, 0] = jnp.concatenate([turned[:DIM].astype(BF16), zero], 0)
        qt_s[n, 1] = jnp.concatenate([zero, turned[DIM:].astype(BF16)], 0)
        forward(n, 1)
        return 0

    lax.fori_loop(0, NEAR, centre, 0)
    passes_along(0)
    kv_along(2, lambda c: c.start())

    def dkv_copy(n, dt, u):
        term = 3 if u == 2 else 1 - dt
        return pltpu.make_async_remote_copy(
            src_ref=dkv.at[n, 3 * (dt + 1) + u], dst_ref=terms.at[3 * core + n, term],
            send_sem=dkv_send.at[n, 3 * (dt + 1) + u], recv_sem=dkv_recv.at[3 * core + n, term],
            device_id={"tm": t + dt, "height": heights[u]}, device_id_type=MESH,
        )

    def over_copy(n, dt):
        return pltpu.make_async_remote_copy(
            src_ref=dkv.at[n, 3 * (dt + 1) + 2], dst_ref=y_back.at[(dt + 1) // 2],
            send_sem=dkv_send.at[n, 3 * (dt + 1) + 2], recv_sem=y_recv.at[(dt + 1) // 2],
            device_id={"height": 2 * (1 - hi) + core}, device_id_type=MESH,
        )

    def along_copy(n, dt):
        return pltpu.make_async_remote_copy(
            src_ref=dkv.at[n, 3 * (dt + 1) + 2], dst_ref=z_back.at[n, (1 - dt) // 2],
            send_sem=dkv_send.at[n, 3 * (dt + 1) + 2], recv_sem=z_recv.at[n, (1 - dt) // 2],
            device_id={"tm": t + dt}, device_id_type=MESH,
        )

    def add_along(n):
        for i, dt in enumerate((-1, 1)):
            @pl.when(has[dt])
            def _():
                pltpu.make_async_remote_copy(
                    src_ref=dkv.at[0, 0], dst_ref=z_back.at[n, i], send_sem=dkv_send.at[0, 0],
                    recv_sem=z_recv.at[n, i], device_id={"height": sibling}, device_id_type=MESH,
                ).wait_recv()
        dkv[n, 5] = (dkv[n, 5].astype(F32) + z_back[n, 0].astype(F32) + z_back[n, 1].astype(F32)).astype(BF16)
        dkv_copy(n, 0, 2).start()

    def add_over(n):
        for i, dt in enumerate((-1, 1)):
            @pl.when(has[dt])
            def _():
                pltpu.make_async_remote_copy(
                    src_ref=dkv.at[0, 0], dst_ref=y_back.at[i], send_sem=dkv_send.at[0, 0],
                    recv_sem=y_recv.at[i], device_id={"height": sibling}, device_id_type=MESH,
                ).wait_recv()
                slot = 3 * (dt + 1) + 1
                dkv[n, slot] = (dkv[n, slot].astype(F32) + y_back[i].astype(F32)).astype(BF16)
                dkv_copy(n, dt, 1).start()

    def dkv_near_copy(n):
        return pltpu.make_async_remote_copy(
            src_ref=dkv.at[n, 4 - inner], dst_ref=terms.at[3 * core + n, 1],
            send_sem=dkv_send.at[n, 4], recv_sem=dkv_recv.at[3 * core + n, 1],
            device_id={"height": sibling}, device_id_type=MESH,
        )

    def oq_copy(n):
        return pltpu.make_async_remote_copy(
            src_ref=oq.at[n, 1 - inner], dst_ref=oq_all.at[3 * core + n],
            send_sem=oq_send.at[n], recv_sem=oq_recv.at[n],
            device_id={"height": sibling}, device_id_type=MESH,
        )

    def backward(n, group):
        first = 0 if group < 3 else TILE
        size = 768 if group < 3 else 1152
        js = slots(group)
        product = jnp.dot(keys(n, group), qt_s[n, 1, :, first:], preferred_element_type=F32)
        e = e_s[n, group] if group < 3 else eh_s[...]
        weights = e.astype(F32) * m_s[n, group:group + 1, first:]
        slopes = (weights * (product - m_s[n, 4:5, first:])).astype(BF16)
        ds_s[:size, first:] = slopes
        w_s[:size, first:] = weights.astype(BF16)
        turned = jnp.concatenate([kvt_s[n, j, :DIM] for j in js], 1)
        part = jnp.dot(turned, slopes, preferred_element_type=F32)
        if group == 3:
            dqt_s[n, :, :TILE] = jnp.zeros((DIM, TILE), F32)
            dqt_s[n, :, TILE:] = part
        else:
            dqt_s[n, :, first:] += part
        rhs = qd[n].reshape(2 * TILE, 2 * DIM)[first:]
        key_part = jnp.dot(ds_s[:size, first:], rhs, preferred_element_type=F32)
        value_part = jnp.dot(w_s[:size, first:], rhs, preferred_element_type=F32)
        lanes = lax.broadcasted_iota(jnp.int32, (size, 2 * DIM), 1)
        both = jnp.where(lanes < DIM, key_part, value_part)
        both = both.astype(BF16)
        for i, j in enumerate(js):
            dkv[n, j] = both[i * TILE:(i + 1) * TILE]

    def groups(n):
        for dt in (-1, 1):
            @pl.when(has[dt])
            def _():
                wait_kv(n, 3 * (dt + 1))
                wait_kv(n, 3 * (dt + 1) + 1)

            @pl.when(has[dt] & (n == 1))
            def _():
                pass_over(1, dt).start()
            forward(n, dt + 1)
            if dt < 0:
                @pl.when(n == 1)
                def _():
                    passes_along(2)

    def head(n):
        @pl.when(n == 1)
        def _():
            wait_kv(n, 5)
        for dt in (-1, 1):
            @pl.when(has[dt])
            def _():
                wait_kv(n, 3 * (dt + 1) + 2)
        forward(n, 3)
        m_s[n, 3:4, :TILE] = jnp.full((1, TILE), -FAR, F32)
        l_s[n, 3:4, :TILE] = jnp.zeros((1, TILE), F32)
        tops = m_s[n, 0:4]
        shares = jnp.exp(tops - jnp.max(tops, axis=0, keepdims=True))
        shares = shares / jnp.sum(shares * l_s[n, 0:4], axis=0, keepdims=True)
        out = ot_s[n, 0] * shares[0:1] + ot_s[n, 1] * shares[1:2] + ot_s[n, 2] * shares[2:3]
        out = jnp.concatenate([out[:, :TILE], out[:, TILE:] + ot_s[n, 3, :, TILE:] * shares[3:4, TILE:]], 1)
        out = out.astype(BF16).astype(F32)
        ot_s[n, 0] = out
        m_s[n, 0:4] = shares
        m_s[n, 4:5] = jnp.sum(qt_s[n, 1, DIM:].astype(F32) * out, axis=0, keepdims=True)

        @pl.when(n == 1)
        def _():
            add_along(0)

        backward(n, 3)
        for dt in (-1, 1):
            @pl.when(has[dt] & (n < 2))
            def _():
                along_copy(n, dt).start()

            @pl.when(has[dt] & (n == 2))
            def _():
                over_copy(n, dt).start()

    def sides(n, _):
        for dt in (-1, 1):
            backward(n, dt + 1)

            @pl.when(has[dt])
            def _():
                dkv_copy(n, dt, 0).start()

            @pl.when(has[dt] & (n < 2))
            def _():
                dkv_copy(n, dt, 1).start()
        return 0

    def step(i, _):
        @pl.when(i < NEAR)
        def _():
            groups(i)

        @pl.when(i > 0)
        def _():
            head(i - 1)
        lax.fori_loop(jnp.where(i == NEAR, 1, 0), jnp.where(i == NEAR, NEAR, i % 2), sides, 0)
        return 0

    lax.fori_loop(0, NEAR + 1, step, 0)

    def last(n, _):
        @pl.when(n == 0)
        def _():
            add_along(1)

        @pl.when(n == 1)
        def _():
            dkv_copy(2, 0, 2).start()
            add_over(2)
        backward(n, 1)
        dkv_near_copy(n).start()
        terms[3 * core + n, 1] = dkv[n, 3 + inner]
        both = jnp.concatenate([ot_s[n, 0], dqt_s[n] * 0.125], 0).T.astype(BF16)
        oq[n, 0] = both[:TILE]
        oq[n, 1] = both[TILE:]
        oq_copy(n).start()
        oq_all[3 * core + n] = oq[n, inner]
        return 0

    lax.fori_loop(0, NEAR, last, 0)

    def wait_terms(n):
        wait_term(3 * (1 - core) + n, 1)
        for c in range(2):
            for dt in (-1, 1):
                @pl.when(has[dt])
                def _():
                    wait_term(3 * c + n, 1 + dt)

            @pl.when(inner == 1)
            def _():
                wait_term(3 * c + n, 3)

    def wait_term(n, term):
        pltpu.make_async_remote_copy(
            src_ref=dkv.at[0, 0], dst_ref=terms.at[n, term], send_sem=dkv_send.at[0, 0], recv_sem=dkv_recv.at[n, term],
            device_id={"height": sibling}, device_id_type=MESH,
        ).wait_recv()

    def store(pair, even, odd, a, b):
        cols = slice(pair * 2 * DIM, (pair + 1) * 2 * DIM)
        a[:, cols] = jnp.where(low, even, swap_halves(odd)).astype(BF16)
        b[:, cols] = jnp.where(low, swap_halves(even), odd).astype(BF16)

    def summed(n, from_partner):
        total = terms[n, 0].astype(F32)
        for i in range(1, 4 if from_partner else 3):
            total = total + terms[n, i].astype(F32)
        return total

    def store_sums(pair):
        for side in range(2):
            @pl.when(inner == side)
            def _():
                store(pair, summed(2 * pair, side), summed(2 * pair + 1, side), kg_ref, vg_ref)

    for n in range(NEAR):
        pltpu.make_async_remote_copy(
            src_ref=oq.at[n, 0], dst_ref=oq_all.at[3 * (1 - core) + n], send_sem=oq_send.at[n], recv_sem=oq_recv.at[n],
            device_id={"height": sibling}, device_id_type=MESH,
        ).wait_recv()
    for pair in range(HEADS // 2):
        store(pair, oq_all[2 * pair].astype(F32), oq_all[2 * pair + 1].astype(F32), att_ref, qg_ref)
    wait_terms(0)
    wait_terms(1)
    store_sums(0)
    wait_terms(2)
    store_sums(1)
    store_sums(2)

    def drain(n, _):
        qd_copy(n).wait_send()
        kv_beside(n, lambda c: c.wait_send())
        kv_along(n, lambda c: c.wait_send())
        for dt in (-1, 1):
            @pl.when(has[dt])
            def _():
                for u in range(3):
                    dkv_copy(n, dt, u).wait_send()

                pass_over(n, dt).wait_send()
        dkv_copy(n, 0, 2).wait_send()
        dkv_near_copy(n).wait_send()
        oq_copy(n).wait_send()
        return 0

    lax.fori_loop(0, NEAR, drain, 0)


def handed_on(*refs):
    copies = [pltpu.make_async_copy(refs[i], refs[4 + i], refs[8].at[i]) for i in range(4)]
    for copy in copies:
        copy.start()
    for copy in copies:
        copy.wait()


def local(tiles_t, queries, key_tokens, value_tokens, cotangent, window_mask):
    flat = (TILE, HEADS * DIM)
    anywhere = pl.BlockSpec(memory_space=pl.ANY)
    block = (TILE, 2 * DIM)
    dma = pltpu.SemaphoreType.DMA
    outs = pl.pallas_call(
        functools.partial(kernel, tiles_t),
        out_shape=[pltpu.VMEM(flat, BF16)] * 4,
        in_specs=[anywhere] * 5,
        out_specs=[pl.BlockSpec(memory_space=pltpu.VMEM)] * 4,
        scratch_shapes=[
            pltpu.VMEM((4, *flat), BF16),
            pltpu.VMEM((9, 4, tiles_t), jnp.int32),
            pltpu.VMEM((2, 9, 1, 2 * DIM), F32),
            pltpu.VMEM((HEADS, *block), BF16),
            pltpu.VMEM((HEADS, *block), BF16),
            pltpu.VMEM((NEAR, 9, *block), BF16),
            pltpu.VMEM((NEAR, 2, *block), BF16),
            pltpu.VMEM((NEAR, 9, *block), BF16),
            pltpu.VMEM((2, *block), BF16),
            pltpu.VMEM((2, 2, *block), BF16),
            pltpu.VMEM((HEADS, 4, *block), BF16),
            pltpu.VMEM((NEAR, 2, *block), BF16),
            pltpu.VMEM((HEADS, *block), BF16),
            pltpu.VMEM((NEAR, 3, 768, 768), BF16),
            pltpu.VMEM((1152, 384), BF16),
            pltpu.VMEM((1152, 768), BF16),
            pltpu.VMEM((1152, 768), BF16),
            pltpu.VMEM((NEAR, 4, DIM, 768), F32),
            pltpu.VMEM((NEAR, 8, 768), F32),
            pltpu.VMEM((NEAR, 8, 768), F32),
            pltpu.VMEM((NEAR, 2, 2 * DIM, 768), BF16),
            pltpu.VMEM((NEAR, DIM, 768), F32),
            pltpu.VMEM((NEAR, 9, 2 * DIM, TILE), BF16),
            dma((5,)),
            dma((NEAR, 7)),
            dma((NEAR, 9)),
            dma((NEAR, 2)),
            dma((NEAR,)),
            dma((NEAR,)),
            dma((NEAR, 9)),
            dma((HEADS, 4)),
            dma((2,)),
            dma((2, 2)),
            dma((NEAR,)),
            dma((NEAR,)),
        ],
        compiler_params=pltpu.CompilerParams(
            collective_id=0, has_side_effects=True, vmem_limit_bytes=56 * 1024 * 1024
        ),
    )(
        window_mask.transpose(2, 1, 0),
        queries.reshape(flat), key_tokens.reshape(flat), value_tokens.reshape(flat), cotangent.reshape(flat),
    )
    outs = pl.pallas_call(
        handed_on,
        out_shape=[jax.ShapeDtypeStruct(flat, BF16)] * 4,
        in_specs=[pl.BlockSpec(memory_space=pltpu.VMEM)] * 4,
        out_specs=[anywhere] * 4,
        scratch_shapes=[dma((4,))],
    )(*(pltpu.with_memory_space_constraint(out, pltpu.VMEM) for out in outs))
    return tuple(out.reshape(queries.shape) for out in outs)


def solution(mesh):
    spec = P("tm", "height", None, "heads")
    return jax.shard_map(
        functools.partial(local, mesh.shape["tm"]), mesh=mesh, in_specs=(spec,) * 4 + (P(),), out_specs=(spec,) * 4,
        check_vma=False,
    )
```

time: 63.3 us -> 51 us (0.81)
  local copies, waits for them, and re-layouts: 6.24 us -> 0 us
  Pallas kernels: 56.2 us -> 50.3 us
    pallas_call x1 -> x2, Pallas kernels: 56.2 us -> 50.3 us  [the longest x1 49.2 us: local(): pl.pallas_call(functools.partial(kernel, tiles_t), out_shape=[pltpu.VMEM(...]
    unnamed x11 -> x0, local copies, waits for them, and re-layouts: 5.43 us -> none
    reshape x1 -> x0, local copies, waits for them, and re-layouts: 0.81 us -> none  [local(): window_mask.reshape(-1)]
where the time goes in v2:
time: 51 us; the launch traced here: 50.9 us
  Pallas kernels  50.3 us (99%)
  between operations  0.64 us (1%)
    pallas_call x1, Pallas kernels, local(): pl.pallas_call(functools.partial(kernel, tiles_t), out_shape=[pltpu.VMEM(...  49.2 us
    pallas_call x1, Pallas kernels, local(): pl.pallas_call(handed_on, out_shape=[jax.ShapeDtypeStruct(flat, BF16)] *...  1.04 us

profile of v2, /device:TPU:7, one launch (start us, length us, event | category | flops | bytes accessed | tf_op | source)
XLA Modules:
  0.0 50.9 jit_solution(66029090908226879)
XLA Ops:
  0.6 49.2 %shard_map.84 = (bf16[384,384]{1,0:T(8,128)(2,1)S(1)}, bf16[384,384]{1,0:T(8,128)(2,1)S(1)}, bf16[384,384]{1,0:T(8,128)(2,1)S(1)}, bf16[384,384]{1,0:T(8,128)(2,1)S(1)}) custom-call(s32[9,4,32]{2,1,0:T(4,128)} %bitcast.13, bf16[384,384]{1,0:T(8,128)(2,1)} %bitcast.9, bf16[384,384]{1,0:T(8,128)(2,1)} %bitcast.10, bf16[384,384]{1,0:T(8,128)(2,1)} %bitcast.11, ...), custom_call_target="tpu_custom_call" | custom-call | tf_op jit(solution)/shard_map/pallas_call | solution.py:492
  49.9 1.0 %shard_map.85 = (bf16[384,384]{1,0:T(8,128)(2,1)}, bf16[384,384]{1,0:T(8,128)(2,1)}, bf16[384,384]{1,0:T(8,128)(2,1)}, bf16[384,384]{1,0:T(8,128)(2,1)}) custom-call(bf16[384,384]{1,0:T(8,128)(2,1)S(1)} %get-tuple-element.12.refs_0_, bf16[384,384]{1,0:T(8,128)(2,1)S(1)} %get-tuple-element.13.refs_1_, bf16[384,384]{1,0:T(8,128)(2,1)S(1)} %get-tuple-element.14.refs_2_, ...), custom_call_target="tpu_custom_call" | custom-call | tf_op jit(solution)/shard_map/pallas_call | solution.py:541

commit v3 on v2

--- a/solution.py
+++ b/solution.py
@@ -66,9 +66,6 @@
         return 0
 
     lax.fori_loop(0, HEADS // 2, functools.partial(pack, kv_own, 0, 1.0), 0)
-    for load in loads[2:]:
-        load.wait()
-    lax.fori_loop(0, HEADS // 2, functools.partial(pack, qd_own, 2, 0.125), 0)
     for dt in (-1, 1):
         @pl.when(jnp.logical_not(has[dt]))
         def _():
@@ -81,6 +78,65 @@
                 z_back[n, (1 + dt) // 2] = jnp.zeros((TILE, 2 * DIM), BF16)
     for n in range(NEAR):
         kv[n, 3 + inner] = kv_own[3 * core + n]
+    count = 3 + 2 * ((t > 0).astype(jnp.int32) + (t < tiles_t - 1).astype(jnp.int32))
+    pl.semaphore_wait(barrier, count)
+
+    def qd_copy(n):
+        return pltpu.make_async_remote_copy(
+            src_ref=qd_own.at[3 * (1 - core) + n], dst_ref=qd.at[n, inner],
+            send_sem=qd_send.at[n], recv_sem=qd_recv.at[n],
+            device_id={"height": sibling}, device_id_type=MESH,
+        )
+
+    def kv_copy(n, dt, to, far=0):
+        slot = 3 * (1 - dt) + (2 if far else inner)
+        index = 5 + to if far else {-1: to, 0: 2, 1: 3 + to}[dt]
+        return pltpu.make_async_remote_copy(
+            src_ref=kv_own.at[3 * to + n], dst_ref=kv.at[n, slot],
+            send_sem=kv_send.at[n, index], recv_sem=kv_recv.at[n, slot],
+            device_id={"tm": t + dt, "height": 2 * (1 - hi if far else hi) + to}, device_id_type=MESH,
+        )
+
+    def kv_along(n, act):
+        for dt in (-1, 1):
+            @pl.when(has[dt])
+            def _():
+                for to in range(2):
+                    act(kv_copy(n, dt, to))
+
+    def kv_beside(n, act):
+        act(kv_copy(n, 0, 1 - core))
+
+        @pl.when(inner == 1)
+        def _():
+            for to in range(2):
+                act(kv_copy(n, 0, to, 1))
+
+    def pass_over(n, dt):
+        slot = 3 * (dt + 1)
+        return pltpu.make_async_remote_copy(
+            src_ref=kv.at[n, slot + 1], dst_ref=kv.at[n, slot + 2],
+            send_sem=pass_send.at[n, (dt + 1) // 2], recv_sem=kv_recv.at[n, slot + 2],
+            device_id={"height": 2 * (1 - hi) + core}, device_id_type=MESH,
+        )
+
+    def pass_along(n, dt):
+        slot = 3 * (1 - dt) + 2
+        return pltpu.make_async_remote_copy(
+            src_ref=kv.at[n, 5], dst_ref=kv.at[n, slot],
+            send_sem=pass_send.at[n, (dt + 1) // 2], recv_sem=kv_recv.at[n, slot],
+            device_id={"tm": t + dt}, device_id_type=MESH,
+        )
+
+    kv_along(0, lambda c: c.start())
+    for n in range(NEAR):
+        kv_beside(n, lambda c: c.start())
+    kv_along(1, lambda c: c.start())
+    for load in loads[2:]:
+        load.wait()
+    lax.fori_loop(0, HEADS // 2, functools.partial(pack, qd_own, 2, 0.125), 0)
+    for n in range(NEAR):
+        qd_copy(n).start()
         qd[n, inner] = qd_own[3 * core + n]
     spot = lax.broadcasted_iota(jnp.int32, (9, 4, tiles_t), 2)
     row = lax.broadcasted_iota(jnp.int32, (9, 4, tiles_t), 1)
@@ -89,66 +145,6 @@
         chosen = jnp.sum(jnp.sum(chosen, axis=2, keepdims=True), axis=1, keepdims=True)
         flag_s[i] = jnp.broadcast_to(chosen, (9, 1, 2 * DIM))
 
-    count = 3 + 2 * ((t > 0).astype(jnp.int32) + (t < tiles_t - 1).astype(jnp.int32))
-    pl.semaphore_wait(barrier, count)
-
-    def qd_copy(n):
-        return pltpu.make_async_remote_copy(
-            src_ref=qd_own.at[3 * (1 - core) + n], dst_ref=qd.at[n, inner],
-            send_sem=qd_send.at[n], recv_sem=qd_recv.at[n],
-            device_id={"height": sibling}, device_id_type=MESH,
-        )
-
-    def kv_copy(n, dt, to, far=0):
-        slot = 3 * (1 - dt) + (2 if far else inner)
-        index = 5 + to if far else {-1: to, 0: 2, 1: 3 + to}[dt]
-        return pltpu.make_async_remote_copy(
-            src_ref=kv_own.at[3 * to + n], dst_ref=kv.at[n, slot],
-            send_sem=kv_send.at[n, index], recv_sem=kv_recv.at[n, slot],
-            device_id={"tm": t + dt, "height": 2 * (1 - hi if far else hi) + to}, device_id_type=MESH,
-        )
-
-    def kv_along(n, act):
-        for dt in (-1, 1):
-            @pl.when(has[dt])
-            def _():
-                for to in range(2):
-                    act(kv_copy(n, dt, to))
-
-    def kv_beside(n, act):
-        act(kv_copy(n, 0, 1 - core))
-
-        @pl.when(inner == 1)
-        def _():
-            for to in range(2):
-                act(kv_copy(n, 0, to, 1))
-
-    def pass_over(n, dt):
-        slot = 3 * (dt + 1)
-        return pltpu.make_async_remote_copy(
-            src_ref=kv.at[n, slot + 1], dst_ref=kv.at[n, slot + 2],
-            send_sem=pass_send.at[n, (dt + 1) // 2], recv_sem=kv_recv.at[n, slot + 2],
-            device_id={"height": 2 * (1 - hi) + core}, device_id_type=MESH,
-        )
-
-    def pass_along(n, dt):
-        slot = 3 * (1 - dt) + 2
-        return pltpu.make_async_remote_copy(
-            src_ref=kv.at[n, 5], dst_ref=kv.at[n, slot],
-            send_sem=pass_send.at[n, (dt + 1) // 2], recv_sem=kv_recv.at[n, slot],
-            device_id={"tm": t + dt}, device_id_type=MESH,
-        )
-
-    def send_head(n, _):
-        qd_copy(n).start()
-        kv_beside(n, lambda c: c.start())
-
-        @pl.when(n < 2)
-        def _():
-            kv_along(n, lambda c: c.start())
-        return 0
-
-    lax.fori_loop(0, NEAR, send_head, 0)
 
     def wait_kv(n, slot):
         pltpu.make_async_remote_copy(
@@ -187,7 +183,7 @@
         js = slots(group)
         first = 0 if group < 3 else TILE
         for j in js:
-            kvt_s[n, j] = kv[n, j].astype(F32).T.astype(BF16)
+            kvt_s[n, j] = kv[n, j].T
         scores = jnp.dot(keys(n, group), qt_s[n, 0, :, first:], preferred_element_type=F32)
         flags = [allowed(j // 3 - 1, j % 3) > 0 for j in js]
         tops = [
@@ -223,7 +219,6 @@
 
     lax.fori_loop(0, NEAR, centre, 0)
     passes_along(0)
-    kv_along(2, lambda c: c.start())
 
     def dkv_copy(n, dt, u):
         term = 3 if u == 2 else 1 - dt
@@ -285,18 +280,20 @@
         )
 
     def backward(n, group):
-        first = 0 if group < 3 else TILE
-        size = 768 if group < 3 else 1152
-        js = slots(group)
-        product = jnp.dot(keys(n, group), qt_s[n, 1, :, first:], preferred_element_type=F32)
-        e = e_s[n, group] if group < 3 else eh_s[...]
-        weights = e.astype(F32) * m_s[n, group:group + 1, first:]
+        halo = isinstance(group, int) and group == 3
+        first, size = (TILE, 1152) if halo else (0, 768)
+        js = [2, 5, 8] if halo else [3 * group, 3 * group + 1]
+        row = pl.ds(group, 1)
+        tokens = keys(n, 3) if halo else kv[n, pl.ds(3 * group, 2)].reshape(2 * TILE, 2 * DIM)
+        product = jnp.dot(tokens, qt_s[n, 1, :, first:], preferred_element_type=F32)
+        e = eh_s[...] if halo else e_s[n, group]
+        weights = e.astype(F32) * m_s[n, row, first:]
         slopes = (weights * (product - m_s[n, 4:5, first:])).astype(BF16)
         ds_s[:size, first:] = slopes
         w_s[:size, first:] = weights.astype(BF16)
         turned = jnp.concatenate([kvt_s[n, j, :DIM] for j in js], 1)
         part = jnp.dot(turned, slopes, preferred_element_type=F32)
-        if group == 3:
+        if halo:
             dqt_s[n, :, :TILE] = jnp.zeros((DIM, TILE), F32)
             dqt_s[n, :, TILE:] = part
         else:
@@ -325,6 +322,10 @@
                 @pl.when(n == 1)
                 def _():
                     passes_along(2)
+            else:
+                @pl.when(n == 0)
+                def _():
+                    kv_along(2, lambda c: c.start())
 
     def head(n):
         @pl.when(n == 1)
@@ -361,15 +362,19 @@
             def _():
                 over_copy(n, dt).start()
 
+    forward_first = lax.rem(t, 8) == 7
+
     def sides(n, _):
-        for dt in (-1, 1):
+        for k in range(2):
+            dt = jnp.where(forward_first, 1 - 2 * k, 2 * k - 1)
+            there = (t + dt >= 0) & (t + dt < tiles_t)
             backward(n, dt + 1)
 
-            @pl.when(has[dt])
+            @pl.when(there)
             def _():
                 dkv_copy(n, dt, 0).start()
 
-            @pl.when(has[dt] & (n < 2))
+            @pl.when(there & (n < 2))
             def _():
                 dkv_copy(n, dt, 1).start()
         return 0
@@ -443,6 +448,9 @@
             def _():
                 store(pair, summed(2 * pair, side), summed(2 * pair + 1, side), kg_ref, vg_ref)
 
+    wait_terms(0)
+    wait_terms(1)
+    store_sums(0)
     for n in range(NEAR):
         pltpu.make_async_remote_copy(
             src_ref=oq.at[n, 0], dst_ref=oq_all.at[3 * (1 - core) + n], send_sem=oq_send.at[n], recv_sem=oq_recv.at[n],
@@ -450,9 +458,6 @@
         ).wait_recv()
     for pair in range(HEADS // 2):
         store(pair, oq_all[2 * pair].astype(F32), oq_all[2 * pair + 1].astype(F32), att_ref, qg_ref)
-    wait_terms(0)
-    wait_terms(1)
-    store_sums(0)
     wait_terms(2)
     store_sums(1)
     store_sums(2)

time: 51 us -> 49.9 us (0.978)
  Pallas kernels: 50.3 us -> 49.2 us
    pallas_call x1, Pallas kernels: 49.2 us -> 48.1 us  [local(): pl.pallas_call(functools.partial(kernel, tiles_t), out_shape=[pltpu.VMEM(...]
where the time goes in v3:
time: 49.9 us; the launch traced here: 49.8 us
  Pallas kernels  49.2 us (99%)
  between operations  0.64 us (1%)
    pallas_call x1, Pallas kernels, local(): pl.pallas_call(functools.partial(kernel, tiles_t), out_shape=[pltpu.VMEM(...  48.1 us
    pallas_call x1, Pallas kernels, local(): pl.pallas_call(handed_on, out_shape=[jax.ShapeDtypeStruct(flat, BF16)] *...  1.04 us

profile of v3, /device:TPU:7, one launch (start us, length us, event | category | flops | bytes accessed | tf_op | source)
XLA Modules:
  0.0 49.8 jit_solution(2068869137487672228)
XLA Ops:
  0.6 48.1 %shard_map.84 = (bf16[384,384]{1,0:T(8,128)(2,1)S(1)}, bf16[384,384]{1,0:T(8,128)(2,1)S(1)}, bf16[384,384]{1,0:T(8,128)(2,1)S(1)}, bf16[384,384]{1,0:T(8,128)(2,1)S(1)}) custom-call(s32[9,4,32]{2,1,0:T(4,128)} %bitcast.13, bf16[384,384]{1,0:T(8,128)(2,1)} %bitcast.9, bf16[384,384]{1,0:T(8,128)(2,1)} %bitcast.10, bf16[384,384]{1,0:T(8,128)(2,1)} %bitcast.11, ...), custom_call_target="tpu_custom_call" | custom-call | tf_op jit(solution)/shard_map/pallas_call | solution.py:497
  48.8 1.0 %shard_map.85 = (bf16[384,384]{1,0:T(8,128)(2,1)}, bf16[384,384]{1,0:T(8,128)(2,1)}, bf16[384,384]{1,0:T(8,128)(2,1)}, bf16[384,384]{1,0:T(8,128)(2,1)}) custom-call(bf16[384,384]{1,0:T(8,128)(2,1)S(1)} %get-tuple-element.12.refs_0_, bf16[384,384]{1,0:T(8,128)(2,1)S(1)} %get-tuple-element.13.refs_1_, bf16[384,384]{1,0:T(8,128)(2,1)S(1)} %get-tuple-element.14.refs_2_, ...), custom_call_target="tpu_custom_call" | custom-call | tf_op jit(solution)/shard_map/pallas_call | solution.py:546

commit v4 on v3

--- a/solution.py
+++ b/solution.py
@@ -448,16 +448,24 @@
             def _():
                 store(pair, summed(2 * pair, side), summed(2 * pair + 1, side), kg_ref, vg_ref)
 
-    wait_terms(0)
-    wait_terms(1)
-    store_sums(0)
-    for n in range(NEAR):
+    def wait_oq(n):
         pltpu.make_async_remote_copy(
             src_ref=oq.at[n, 0], dst_ref=oq_all.at[3 * (1 - core) + n], send_sem=oq_send.at[n], recv_sem=oq_recv.at[n],
             device_id={"height": sibling}, device_id_type=MESH,
         ).wait_recv()
-    for pair in range(HEADS // 2):
+
+    def store_oq(pair):
         store(pair, oq_all[2 * pair].astype(F32), oq_all[2 * pair + 1].astype(F32), att_ref, qg_ref)
+
+    wait_oq(0)
+    wait_oq(1)
+    store_oq(0)
+    wait_terms(0)
+    wait_terms(1)
+    store_sums(0)
+    wait_oq(2)
+    store_oq(1)
+    store_oq(2)
     wait_terms(2)
     store_sums(1)
     store_sums(2)

time: 49.9 us -> 50 us (level)
  no operation moved by 1% of the time
where the time goes in v4:
time: 50 us; the launch traced here: 49.9 us
  Pallas kernels  49.2 us (98%)
  between operations  0.64 us (1%)
    pallas_call x1, Pallas kernels, local(): pl.pallas_call(functools.partial(kernel, tiles_t), out_shape=[pltpu.VMEM(...  48.2 us
    pallas_call x1, Pallas kernels, local(): pl.pallas_call(handed_on, out_shape=[jax.ShapeDtypeStruct(flat, BF16)] *...  1.04 us

profile of v4, /device:TPU:7, one launch (start us, length us, event | category | flops | bytes accessed | tf_op | source)
XLA Modules:
  0.0 49.9 jit_solution(1756748661407667415)
XLA Ops:
  0.6 48.2 %shard_map.84 = (bf16[384,384]{1,0:T(8,128)(2,1)S(1)}, bf16[384,384]{1,0:T(8,128)(2,1)S(1)}, bf16[384,384]{1,0:T(8,128)(2,1)S(1)}, bf16[384,384]{1,0:T(8,128)(2,1)S(1)}) custom-call(s32[9,4,32]{2,1,0:T(4,128)} %bitcast.13, bf16[384,384]{1,0:T(8,128)(2,1)} %bitcast.9, bf16[384,384]{1,0:T(8,128)(2,1)} %bitcast.10, bf16[384,384]{1,0:T(8,128)(2,1)} %bitcast.11, ...), custom_call_target="tpu_custom_call" | custom-call | tf_op jit(solution)/shard_map/pallas_call | solution.py:505
  48.8 1.0 %shard_map.85 = (bf16[384,384]{1,0:T(8,128)(2,1)}, bf16[384,384]{1,0:T(8,128)(2,1)}, bf16[384,384]{1,0:T(8,128)(2,1)}, bf16[384,384]{1,0:T(8,128)(2,1)}) custom-call(bf16[384,384]{1,0:T(8,128)(2,1)S(1)} %get-tuple-element.12.refs_0_, bf16[384,384]{1,0:T(8,128)(2,1)S(1)} %get-tuple-element.13.refs_1_, bf16[384,384]{1,0:T(8,128)(2,1)S(1)} %get-tuple-element.14.refs_2_, ...), custom_call_target="tpu_custom_call" | custom-call | tf_op jit(solution)/shard_map/pallas_call | solution.py:554
